TPU v7x, 128 devices: a whole 4x4x4 slice. The times are simulated.
128 devices in a mesh: grp: 4 (over z), sub: 32 (over x, y, core).
Axes of the slice: x: 4, y: 4, z: 4, core: 2. Of those that a mesh axis runs over, the one named last changes fastest.
Arguments:
- deformation_vector: float32 [3, 128, 1024, 256], P(None, 'grp', 'sub'), may hold values from -6 to 6
- heating_traction: float32 [3, 128, 1024, 256], P(None, 'grp', 'sub'), may hold values from -6 to 6
- heat_level: float32 [128, 1024, 256], P('grp', 'sub'), may hold values from 0 to 1
- substance_label: int32 [128, 1024, 256], P('grp', 'sub'), may hold values from 0 to 3
- substance_stiffness_list: float32 [4, 2], replicated, may hold values from 0.3 to 3
- subregion_spans: int32 [4, 32], P('grp', 'sub'), may hold values from 64 to 256, as said below
- projection_basis: bfloat16 [8, 3, 128, 1024, 256], P(None, None, 'grp', 'sub'), may hold values from -0.0068359375 to 0.0068359375
- reduced_system_reciprocal: float32 [1024, 1024], P(('grp', 'sub')), may hold values from -1 to 1
Outputs:
- displacement_next: float32 [3, 128, 1024, 256], P(None, 'grp', 'sub')
- residual: float32 [3, 128, 1024, 256], P(None, 'grp', 'sub')
- coarse_update: float32 [1024], P(('grp', 'sub'))
Inputs may be any that keep to these rules, and one draw needn't show every extreme that they name: `subregion_spans`: some subdomain is active along its whole third dimension.
All inputs are finite; a program needn't handle non-finite values.
Results may differ from a plain program's by a relative error of at most 0.003.
Values sent between devices are 32-bit elements; how exact they have to be, the bound alone decides.
A program may use at most 128 MiB of HBM per device.

v0:
```python
import jax
import jax.numpy as jnp
from jax import lax
from jax.sharding import PartitionSpec as P

SWEEPS = 2


SHIFT = 1.0
ROBIN = 1.0
OMEGA = 0.6
UNITS = ((1, 0, 0), (0, 1, 0), (0, 0, 1))


def with_halo(cells, sides, width):
    for axis, dim in sides:
        count = lax.axis_size(axis)
        ends = count - 1
        head = lax.slice_in_dim(cells, 0, width, axis=dim)
        tail = lax.slice_in_dim(cells, cells.shape[dim] - width, cells.shape[dim], axis=dim)
        cells = jnp.concatenate(
            [
                lax.ppermute(tail, axis, [(i, (i + 1) % count) for i in range(ends)]),
                cells,
                lax.ppermute(head, axis, [((i + 1) % count, i) for i in range(ends)]),
            ],
            axis=dim,
        )
    return cells


def combine(first, second, sign):
    return tuple((left + sign * right for left, right in zip(first, second)))


def negate(first):
    return tuple((-left for left in first))


def stencil(padded, rigidity_amount, lambda_stiffness):
    size_x, size_y, size_z = rigidity_amount.shape

    def pick(component, offset):
        return padded[
            component,
            1 + offset[0] : 1 + offset[0] + size_x,
            1 + offset[1] : 1 + offset[1] + size_y,
            1 + offset[2] : 1 + offset[2] + size_z,
        ]

    results = []
    for component in range(3):
        center = pick(component, (0, 0, 0))
        laplace = -6.0 * center
        graddiv = jnp.zeros_like(center)
        for direction in range(3):
            forward = pick(component, UNITS[direction])
            backward = pick(component, negate(UNITS[direction]))
            laplace = laplace + forward + backward
            if direction == component:
                graddiv = graddiv + (forward + backward - 2.0 * center)
            else:
                own_unit = UNITS[component]
                other = UNITS[direction]
                cross = pick(direction, combine(own_unit, other, 1)) - pick(
                    direction, combine(own_unit, other, -1)
                )
                cross = (
                    cross
                    - pick(direction, combine(negate(own_unit), other, 1))
                    + pick(direction, combine(negate(own_unit), other, -1))
                )
                graddiv = graddiv + 0.25 * cross
        results.append(
            SHIFT * center
            - rigidity_amount * laplace
            - (lambda_stiffness + rigidity_amount) * graddiv
        )
    return jnp.stack(results)


def operate(field, rigidity_amount, lambda_stiffness):
    return stencil(
        jnp.pad(field, ((0, 0), (1, 1), (1, 1), (1, 1))), rigidity_amount, lambda_stiffness
    )


def block_masks(shape):
    index_x = lax.broadcasted_iota(jnp.int32, shape, 0)
    index_y = lax.broadcasted_iota(jnp.int32, shape, 1)
    inner = (index_x >= 1) & (index_x <= shape[0] - 2) & (index_y >= 1) & (index_y <= shape[1] - 2)
    edge = (index_x == 1) | (index_x == shape[0] - 2) | (index_y == 1) | (index_y == shape[1] - 2)
    rim = jnp.where(inner & edge, 1.0, 0.0).astype(jnp.float32)
    return (inner, rim)


def stiffness_constants(substance_label, heat_level, stiffness_lookup, enabled_marker):
    rigidity_amount = jnp.zeros(substance_label.shape, jnp.float32)
    lambda_stiffness = jnp.zeros(substance_label.shape, jnp.float32)
    for index in range(stiffness_lookup.shape[0]):
        rigidity_amount = jnp.where(
            substance_label == index, stiffness_lookup[index, 0], rigidity_amount
        )
        lambda_stiffness = jnp.where(
            substance_label == index, stiffness_lookup[index, 1], lambda_stiffness
        )
    weakening_multiplier = 2.0 - heat_level
    rigidity_amount = jnp.where(enabled_marker, rigidity_amount * weakening_multiplier, 0.0)
    lambda_stiffness = jnp.where(enabled_marker, lambda_stiffness * weakening_multiplier, 0.0)
    return (rigidity_amount, lambda_stiffness)


def solve_direct(state, width):
    started = state[0:3]
    forcing = state[3:6]
    rigidity_amount = state[6]
    lambda_stiffness = state[7]
    inner, rim = block_masks(rigidity_amount.shape)
    update = inner & (rigidity_amount > 0)
    scale = SHIFT + 8.0 * rigidity_amount + 2.0 * lambda_stiffness + ROBIN * rim
    field = started
    for sweep_step in range(width):
        defect = (
            forcing
            - operate(field, rigidity_amount, lambda_stiffness)
            - ROBIN * rim * (field - started)
        )
        field = jnp.where(update, field + OMEGA * defect / scale, field)
    return field[:, width:-width, width:-width, :]


def shards(
    deformation_vector,
    heating_traction,
    heat_level,
    substance_label,
    substance_stiffness_list,
    subregion_spans,
    projection_basis,
    reduced_system_reciprocal,
):
    depth = lax.broadcasted_iota(jnp.int32, substance_label.shape, 2)
    enabled_marker = depth < subregion_spans[0, 0]
    rigidity_amount, lambda_stiffness = stiffness_constants(
        substance_label, heat_level, substance_stiffness_list, enabled_marker
    )
    started = jnp.where(enabled_marker, deformation_vector, 0.0)
    forcing = jnp.where(enabled_marker, heating_traction, 0.0)
    state = jnp.concatenate(
        [started, forcing, rigidity_amount[None], lambda_stiffness[None]], axis=0
    )
    margin = with_halo(state, (("grp", 1), ("sub", 2)), SWEEPS)
    moved = solve_direct(margin, SWEEPS)
    edges_new = with_halo(moved, (("grp", 1), ("sub", 2)), 1)
    applied_new = stencil(
        jnp.pad(edges_new, ((0, 0), (0, 0), (0, 0), (1, 1))), rigidity_amount, lambda_stiffness
    )
    residual = jnp.where(enabled_marker, forcing - applied_new, 0.0)
    residual_half = residual.astype(jnp.bfloat16)
    vectors = projection_basis.reshape(projection_basis.shape[0], -1)
    coarse_local = jnp.dot(vectors, residual_half.reshape(-1), preferred_element_type=jnp.float32)
    gathered = lax.all_gather(coarse_local, ("grp", "sub"), axis=0, tiled=True)
    coarse_update = jnp.dot(reduced_system_reciprocal, gathered, precision=lax.Precision.HIGHEST)
    return (moved, residual, coarse_update)


def solution(mesh):
    placed = (
        P(None, "grp", "sub", None),
        P(None, "grp", "sub", None),
        P("grp", "sub", None),
        P("grp", "sub", None),
        P(),
        P("grp", "sub"),
        P(None, None, "grp", "sub", None),
        P(("grp", "sub"), None),
    )
    return jax.shard_map(
        shards,
        mesh=mesh,
        in_specs=placed,
        out_specs=(P(None, "grp", "sub", None), P(None, "grp", "sub", None), P(("grp", "sub"))),
        check_vma=False,
    )
```

profile of v0, /device:TPU:0, one launch (start us, length us, event | category | flops | bytes accessed | tf_op | source)
XLA Modules:
  0.0 291.0 jit_solution(4623767108774383891)
XLA Ops:
  0.6 1.7 fusion.186
  3.0 4.3 %broadcast_select_fusion.1 = (f32[3,32,32,256]{3,2,1,0:T(8,128)S(1)}, f32[3,32,32,256]{3,2,1,0:T(8,128)S(1)}) fusion(f32[3,32,32,256]{3,2,1,0:T(8,128)} %param.8, pred[256]{0:T(512)(128)(4,1)S(1)} %iota_compare_fusion.2, f32[3,32,32,256]{3,2,1,0:T(8,128)} %param.9), kind=kLoop, calls=%fused_computation.111 | loop fusion | flops 1572864 | bytes 12583168 | tf_op jit(solution)/shard_map/jit(_where)/select_n | solution.py:147
  7.4 3.3 %fusion.183 = (f32[1,32,32,256]{3,2,1,0:T(8,128)S(1)}, pred[32,32,256]{2,1,0:T(8,128)(4,1)S(1)}, pred[32,32,256]{2,1,0:T(8,128)(4,1)S(1)}, pred[32,32,256]{2,1,0:T(8,128)(4,1)S(1)}, pred[32,32,256]{2,1,0:T(8,128)(4,1)S(1)}) fusion(f32[32,32,256]{2,1,0:T(8,128)S(1)} %copy-done.4, f32[]{:T(128)} %bitcast.4, f32[]{:T(128)} %bitcast.3, f32[]{:T(128)} %bitcast.2, ...), kind=kLoop, calls=%fused_computation.349 | loop fusion | flops 2883584 | bytes 4194576 | tf_op jit(solution)/shard_map/broadcast_in_dim | solution.py:150
  10.7 3.1 %fusion.180 = f32[1,32,32,256]{3,2,1,0:T(8,128)S(1)} fusion(f32[32,32,256]{2,1,0:T(8,128)S(1)} %copy-done.4, pred[32,32,256]{2,1,0:T(8,128)(4,1)S(1)} %get-tuple-element.12, pred[32,32,256]{2,1,0:T(8,128)(4,1)S(1)} %get-tuple-element.11, pred[32,32,256]{2,1,0:T(8,128)(4,1)S(1)} %get-tuple-element.10, pred[32,32,256]{2,1,0:T(8,128)(4,1)S(1)} %get-tuple-element.9, ...), kind=kLoop, calls=%fused_computation.341 | loop fusion | flops 1835008 | bytes 3146000 | tf_op jit(solution)/shard_map/broadcast_in_dim | solution.py:150
  13.9 3.9 %collective-permute-start = (f32[8,2,32,256]{3,2,1,0:T(8,128)S(1)}, f32[8,2,32,256]{3,2,1,0:T(8,128)S(1)}, u32[]{:S(2)}, u32[]{:S(2)}) collective-permute-start(f32[8,2,32,256]{3,2,1,0:T(8,128)S(1)} %get-tuple-element.21), channel_id=1, source_target_pairs={{0,32},{32,64},{64,96},{1,33},{33,65},{65,97},{2,34},{34,66},{66,9... | collective-permute-start | bytes 1572872 | tf_op jit(solution)/shard_map/ppermute | solution.py:23
  17.9 1.3 collective-permute-start.1
  19.2 9.8 %collective-permute-done = f32[8,2,32,256]{3,2,1,0:T(8,128)S(1)} collective-permute-done((f32[8,2,32,256]{3,2,1,0:T(8,128)S(1)}, f32[8,2,32,256]{3,2,1,0:T(8,128)S(1)}, u32[]{:S(2)}, u32[]{:S(2)}) %collective-permute-start) | collective-permute-done | bytes 524320 | tf_op jit(solution)/shard_map/ppermute | solution.py:23
  29.0 4.3 %collective-permute-done.1 = f32[8,2,32,256]{3,2,1,0:T(8,128)S(1)} collective-permute-done((f32[8,2,32,256]{3,2,1,0:T(8,128)S(1)}, f32[8,2,32,256]{3,2,1,0:T(8,128)S(1)}, u32[]{:S(2)}, u32[]{:S(2)}) %collective-permute-start.1) | collective-permute-done | bytes 524320 | tf_op jit(solution)/shard_map/ppermute | solution.py:25
  34.2 1.3 collective-permute-start.2
  35.7 1.5 collective-permute-start.3
  38.2 3.2 %collective-permute-done.3 = f32[8,36,2,256]{3,0,2,1:T(8,128)S(1)} collective-permute-done((f32[8,36,2,256]{3,0,2,1:T(8,128)S(1)}, f32[8,36,2,256]{3,0,2,1:T(8,128)S(1)}, u32[]{:S(2)}, u32[]{:S(2)}) %collective-permute-start.3) | collective-permute-done | bytes 589856 | tf_op jit(solution)/shard_map/ppermute | solution.py:25
  41.7 6.0 %pad_maximum_fusion = f32[8,36,36,256]{3,2,1,0:T(8,128)S(1)} fusion(f32[8,36,2,256]{3,2,1,0:T(2,128)S(1)} %copy.37, f32[8,2,32,256]{3,2,1,0:T(8,128)S(1)} %collective-permute-done.1, f32[1,32,32,256]{3,2,1,0:T(8,128)S(1)} %fusion.180, f32[1,32,32,256]{3,2,1,0:T(8,128)S(1)} %get-tuple-element.8, f32[3,32,32,256]{3,2,1,0:T(8,128)S(1)} %get-tuple-element.38, ...), kind=kLoop, calls=%fused_computation.86 | loop fusion | flops 18579456 | bytes 21233664 | tf_op jit(solution)/shard_map/concatenate | solution.py:21
  47.7 2.6 slice.694
  51.1 2.3 copy-done.1
  53.4 1.4 bitcast_and_fusion
  54.8 35.6 %fusion.17 = (f32[1,36,36,256]{3,2,1,0:T(8,128)}, f32[1,36,36,256]{3,2,1,0:T(8,128)}, f32[1,36,36,256]{3,2,1,0:T(8,128)}) fusion(f32[3,36,36,256]{3,2,1,0:T(8,128)} %slice.694, f32[8,36,36,256]{3,2,1,0:T(8,128)} %copy-done.1), kind=kLoop, calls=%fused_computation.118 | loop fusion | flops 23887872 | bytes 14598144 | tf_op jit(solution)/shard_map/sub | solution.py:75
  90.5 7.6 %add_select_fusion.1 = f32[3,36,36,256]{3,2,1,0:T(8,128)} fusion(f32[1,36,36,256]{3,2,1,0:T(8,128)} %get-tuple-element.17, f32[1,36,36,256]{3,2,1,0:T(8,128)} %get-tuple-element.18, f32[1,36,36,256]{3,2,1,0:T(8,128)} %get-tuple-element.16, f32[8,36,36,256]{3,2,1,0:T(8,128)} %copy-done.1, f32[36,36,256]{2,1,0:T(8,128)S(1)} %add_bitcast_fusion, ...), kind=kLoop, calls=%fused_computation.90 | loop fusion | flops 9953280 | bytes 18911232 | tf_op jit(solution)/shard_map/jit(_where)/select_n | solution.py:128
  98.0 36.2 %fusion.74 = (f32[1,36,36,256]{3,2,1,0:T(8,128)}, f32[1,36,36,256]{3,2,1,0:T(8,128)}, f32[1,36,36,256]{3,2,1,0:T(8,128)}) fusion(f32[3,36,36,256]{3,2,1,0:T(8,128)} %add_select_fusion.1, f32[8,36,36,256]{3,2,1,0:T(8,128)} %copy-done.1), kind=kLoop, calls=%fused_computation.175 | loop fusion | flops 23887872 | bytes 15777792 | tf_op jit(solution)/shard_map/sub | solution.py:75
  134.2 7.4 %add_select_fusion = f32[3,36,36,256]{3,2,1,0:T(8,128)S(1)} fusion(f32[1,36,36,256]{3,2,1,0:T(8,128)} %get-tuple-element.14, f32[1,36,36,256]{3,2,1,0:T(8,128)} %get-tuple-element.15, f32[1,36,36,256]{3,2,1,0:T(8,128)} %get-tuple-element.13, f32[8,36,36,256]{3,2,1,0:T(8,128)} %copy-done.1, f32[36,36,256]{2,1,0:T(8,128)S(1)} %add_bitcast_fusion, ...), kind=kLoop, calls=%fused_computation.89 | loop fusion | flops 19906560 | bytes 22892544 | tf_op jit(solution)/shard_map/jit(_where)/select_n | solution.py:128
  141.7 1.3 collective-permute-start.4
  143.0 4.6 %collective-permute-start.5 = (f32[3,1,32,256]{3,2,1,0:T(8,128)S(1)}, f32[3,1,32,256]{3,2,1,0:T(8,128)S(1)}, u32[]{:S(2)}, u32[]{:S(2)}) collective-permute-start(f32[3,1,32,256]{3,2,1,0:T(8,128)S(1)} %get-tuple-element.23), channel_id=1, source_target_pairs={{0,32},{32,64},{64,96},{1,33},{33,65},{65,97},{2,34},{34,66},{66,9... | collective-permute-start | bytes 294920 | tf_op jit(solution)/shard_map/ppermute | solution.py:23
  148.2 1.5 collective-permute-done.5
  151.1 1.3 collective-permute-start.6
  153.1 9.8 %collective-permute-start.7 = (f32[3,34,1,256]{3,1,2,0:T(8,128)}, f32[3,34,1,256]{3,1,2,0:T(8,128)}, u32[]{:S(2)}, u32[]{:S(2)}) collective-permute-start(f32[3,34,1,256]{3,1,2,0:T(8,128)} %copy.40), channel_id=1, source_target_pairs={{0,1},{1,2},{2,3},{3,4},{4,5},{5,6},{6,7},{7,8},{8,9},{9,10},{10,1... | collective-permute-start | bytes 313352 | tf_op jit(solution)/shard_map/ppermute | solution.py:23
  165.3 2.2 pad_maximum_fusion.1
  167.5 4.0 %select_maximum_fusion = f32[3,34,34,258]{3,2,1,0:T(8,128)S(1)} fusion(f32[3,34,1,256]{3,2,1,0:T(1,128)S(1)} %copy.39, f32[3,34,1,256]{3,2,1,0:T(1,128)S(1)} %copy.41, f32[3,1,32,256]{3,2,1,0:T(8,128)S(1)} %collective-permute-done.4, f32[3,32,32,256]{3,2,1,0:T(8,128)S(1)} %slice.703, f32[3,1,32,256]{3,2,1,0:T(8,128)S(1)} %copy-done.14), kind=kLoop, calls=%fused_computation.91 | loop fusion | flops 10736928 | bytes 7130208 | tf_op jit(solution)/shard_map/concatenate | solution.py:21
  171.6 8.5 %fusion.169 = f32[1,32,32,256]{3,2,1,0:T(8,128)S(1)} fusion(f32[3,34,34,258]{3,2,1,0:T(8,128)S(1)} %select_maximum_fusion, f32[3,34,33,256]{3,2,1,0:T(8,128)S(1)} %get-tuple-element.26, f32[3,34,33,256]{3,2,1,0:T(8,128)S(1)} %get-tuple-element.25, f32[3,32,32,256]{3,2,1,0:T(8,128)S(1)} %slice.703, f32[3,1,32,256]{3,2,1,0:T(8,128)S(1)} %copy-done.14, ...), kind=kLoop, calls=%fused_computation.299 | loop fusion | flops 10485760 | bytes 20119840 | tf_op jit(solution)/shard_map/stack | solution.py:79
  180.2 8.4 %fusion.152 = f32[1,32,32,256]{3,2,1,0:T(8,128)S(1)} fusion(f32[3,34,34,258]{3,2,1,0:T(8,128)S(1)} %select_maximum_fusion, f32[3,34,33,256]{3,2,1,0:T(8,128)S(1)} %get-tuple-element.26, f32[3,34,33,256]{3,2,1,0:T(8,128)S(1)} %get-tuple-element.25, f32[3,32,32,256]{3,2,1,0:T(8,128)S(1)} %slice.703, f32[3,1,32,256]{3,2,1,0:T(8,128)S(1)} %copy-done.14, ...), kind=kLoop, calls=%fused_computation.269 | loop fusion | flops 10485760 | bytes 20119840 | tf_op jit(solution)/shard_map/stack | solution.py:79
  188.6 9.0 %fusion.136 = f32[1,32,32,256]{3,2,1,0:T(8,128)S(1)} fusion(f32[3,34,34,258]{3,2,1,0:T(8,128)S(1)} %select_maximum_fusion, f32[3,34,33,256]{3,2,1,0:T(8,128)S(1)} %get-tuple-element.26, f32[3,34,33,256]{3,2,1,0:T(8,128)S(1)} %get-tuple-element.25, f32[3,32,32,256]{3,2,1,0:T(8,128)S(1)} %slice.703, f32[3,1,32,256]{3,2,1,0:T(8,128)S(1)} %copy-done.14, ...), kind=kLoop, calls=%fused_computation.240 | loop fusion | flops 10223616 | bytes 20119840 | tf_op jit(solution)/shard_map/stack | solution.py:79
  197.7 2.8 convert_bitcast_fusion
  200.5 14.3 %fusion.125 = f32[8]{0:T(128)S(1)} fusion(bf16[8,3,32,32,256]{4,3,2,1,0:T(8,128)(2,1)} %param.14, bf16[3,32,32,256,1]{3,2,1,0,4:T(8,128)(2,1)S(1)} %get-tuple-element.6), kind=kOutput, calls=%fused_computation.231 | convolution fusion | flops 12582912 | bytes 14155808 | tf_op jit(solution)/shard_map/dot_general | solution.py:161
  215.0 75.3 %all-reduce.3 = f32[1024]{0:T(1024)S(1)} all-reduce(f32[1024]{0:T(1024)S(1)} %dynamic-update-slice), channel_id=1, replica_groups=mesh['grp'=4,'sub'=32] {'grp','sub'}, use_global_device_ids=true, to_apply=%add.3 | all-reduce | flops 1024 | bytes 8192
  (62 shorter events, 9.1 us)
Async XLA Ops:
  0.6 289.7 %copy-start = (f32[8,1024]{1,0:T(8,128)S(1)}, f32[8,1024]{1,0:T(8,128)}, u32[]{:S(2)}) copy-start(f32[8,1024]{1,0:T(8,128)} %param.15) | copy-start | bytes 98308
  3.0 4.4 %copy-start.4 = (f32[32,32,256]{2,1,0:T(8,128)S(1)}, f32[32,32,256]{2,1,0:T(8,128)}, u32[]{:S(2)}) copy-start(f32[32,32,256]{2,1,0:T(8,128)} %param.10) | copy-start | bytes 3145732
  3.0 4.4 %copy-start.15 = (s32[32,32,256]{2,1,0:T(8,128)S(1)}, s32[32,32,256]{2,1,0:T(8,128)}, u32[]{:S(2)}) copy-start(s32[32,32,256]{2,1,0:T(8,128)} %param.11) | copy-start | bytes 3145732
  10.7 3.1 %copy-start.7 = (pred[32,32,256]{2,1,0:T(8,128)(4,1)}, pred[32,32,256]{2,1,0:T(8,128)(4,1)S(1)}, u32[]{:S(2)}) copy-start(pred[32,32,256]{2,1,0:T(8,128)(4,1)S(1)} %get-tuple-element.10) | copy-start | bytes 786436
  10.7 3.1 %copy-start.9 = (pred[32,32,256]{2,1,0:T(8,128)(4,1)}, pred[32,32,256]{2,1,0:T(8,128)(4,1)S(1)}, u32[]{:S(2)}) copy-start(pred[32,32,256]{2,1,0:T(8,128)(4,1)S(1)} %get-tuple-element.11) | copy-start | bytes 786436
  10.7 3.1 %copy-start.11 = (pred[32,32,256]{2,1,0:T(8,128)(4,1)}, pred[32,32,256]{2,1,0:T(8,128)(4,1)S(1)}, u32[]{:S(2)}) copy-start(pred[32,32,256]{2,1,0:T(8,128)(4,1)S(1)} %get-tuple-element.12) | copy-start | bytes 786436
  13.9 15.1 %collective-permute-start = (f32[8,2,32,256]{3,2,1,0:T(8,128)S(1)}, f32[8,2,32,256]{3,2,1,0:T(8,128)S(1)}, u32[]{:S(2)}, u32[]{:S(2)}) collective-permute-start(f32[8,2,32,256]{3,2,1,0:T(8,128)S(1)} %get-tuple-element.21), channel_id=1, source_target_pairs={{0,32},{32,64},{64,96},{1,33},{33,65},{65,97},{2,34},{34,66},{66,9... | collective-permute-start | bytes 1572872 | tf_op jit(solution)/shard_map/ppermute | solution.py:23
  17.9 15.4 %collective-permute-start.1 = (f32[8,2,32,256]{3,2,1,0:T(8,128)S(1)}, f32[8,2,32,256]{3,2,1,0:T(8,128)S(1)}, u32[]{:S(2)}, u32[]{:S(2)}) collective-permute-start(f32[8,2,32,256]{3,2,1,0:T(8,128)S(1)} %get-tuple-element.22), channel_id=1, source_target_pairs={{32,0},{64,32},{96,64},{33,1},{65,33},{97,65},{34,2},{66,34},{98,6... | collective-permute-start | bytes 1572872 | tf_op jit(solution)/shard_map/ppermute | solution.py:25
  34.2 3.7 %collective-permute-start.2 = (f32[8,36,2,256]{3,0,2,1:T(8,128)S(1)}, f32[8,36,2,256]{3,0,2,1:T(8,128)S(1)}, u32[]{:S(2)}, u32[]{:S(2)}) collective-permute-start(f32[8,36,2,256]{3,0,2,1:T(8,128)S(1)} %copy.34), channel_id=1, source_target_pairs={{0,1},{1,2},{2,3},{3,4},{4,5},{5,6},{6,7},{7,8},{8,9},{9,10},{10,1... | collective-permute-start | bytes 1769480 | tf_op jit(solution)/shard_map/ppermute | solution.py:23
  35.7 5.7 %collective-permute-start.3 = (f32[8,36,2,256]{3,0,2,1:T(8,128)S(1)}, f32[8,36,2,256]{3,0,2,1:T(8,128)S(1)}, u32[]{:S(2)}, u32[]{:S(2)}) collective-permute-start(f32[8,36,2,256]{3,0,2,1:T(8,128)S(1)} %copy.35), channel_id=1, source_target_pairs={{1,0},{2,1},{3,2},{4,3},{5,4},{6,5},{7,6},{8,7},{9,8},{10,9},{11,1... | collective-permute-start | bytes 1769480 | tf_op jit(solution)/shard_map/ppermute | solution.py:25
  47.7 5.7 %copy-start.1 = (f32[8,36,36,256]{3,2,1,0:T(8,128)}, f32[8,36,36,256]{3,2,1,0:T(8,128)S(1)}, u32[]{:S(2)}) copy-start(f32[8,36,36,256]{3,2,1,0:T(8,128)S(1)} %pad_maximum_fusion) | copy-start | bytes 31850500
  141.7 6.4 %copy-start.3 = (f32[3,36,36,256]{3,2,1,0:T(8,128)}, f32[3,36,36,256]{3,2,1,0:T(8,128)S(1)}, u32[]{:S(2)}) copy-start(f32[3,36,36,256]{3,2,1,0:T(8,128)S(1)} %add_select_fusion) | copy-start | bytes 11943940
  141.7 6.5 %collective-permute-start.4 = (f32[3,1,32,256]{3,2,1,0:T(8,128)S(1)}, f32[3,1,32,256]{3,2,1,0:T(8,128)S(1)}, u32[]{:S(2)}, u32[]{:S(2)}) collective-permute-start(f32[3,1,32,256]{3,2,1,0:T(8,128)S(1)} %get-tuple-element.24), channel_id=1, source_target_pairs={{32,0},{64,32},{96,64},{33,1},{65,33},{97,65},{34,2},{66,34},{98,6... | collective-permute-start | bytes 294920 | tf_op jit(solution)/shard_map/ppermute | solution.py:25
  143.0 6.8 %collective-permute-start.5 = (f32[3,1,32,256]{3,2,1,0:T(8,128)S(1)}, f32[3,1,32,256]{3,2,1,0:T(8,128)S(1)}, u32[]{:S(2)}, u32[]{:S(2)}) collective-permute-start(f32[3,1,32,256]{3,2,1,0:T(8,128)S(1)} %get-tuple-element.23), channel_id=1, source_target_pairs={{0,32},{32,64},{64,96},{1,33},{33,65},{65,97},{2,34},{34,66},{66,9... | collective-permute-start | bytes 294920 | tf_op jit(solution)/shard_map/ppermute | solution.py:23
  148.1 40.5 %copy-start.2 = (f32[3,32,32,256]{3,2,1,0:T(8,128)}, f32[3,32,32,256]{3,2,1,0:T(8,128)S(1)}, u32[]{:S(2)}) copy-start(f32[3,32,32,256]{3,2,1,0:T(8,128)S(1)} %slice.703) | copy-start | bytes 9437188
  149.8 0.6 copy-start.13
  151.1 11.8 %collective-permute-start.6 = (f32[3,34,1,256]{3,1,2,0:T(8,128)}, f32[3,34,1,256]{3,1,2,0:T(8,128)}, u32[]{:S(2)}, u32[]{:S(2)}) collective-permute-start(f32[3,34,1,256]{3,1,2,0:T(8,128)} %copy.38), channel_id=1, source_target_pairs={{1,0},{2,1},{3,2},{4,3},{5,4},{6,5},{7,6},{8,7},{9,8},{10,9},{11,1... | collective-permute-start | bytes 313352 | tf_op jit(solution)/shard_map/ppermute | solution.py:25
  153.1 11.0 %collective-permute-start.7 = (f32[3,34,1,256]{3,1,2,0:T(8,128)}, f32[3,34,1,256]{3,1,2,0:T(8,128)}, u32[]{:S(2)}, u32[]{:S(2)}) collective-permute-start(f32[3,34,1,256]{3,1,2,0:T(8,128)} %copy.40), channel_id=1, source_target_pairs={{0,1},{1,2},{2,3},{3,4},{4,5},{5,6},{6,7},{7,8},{8,9},{9,10},{10,1... | collective-permute-start | bytes 313352 | tf_op jit(solution)/shard_map/ppermute | solution.py:23
  162.9 8.7 %slice-start = ((s8[4423680]{0:T(1024)(128)(4,1)}), s8[4194304]{0:T(1024)(128)(4,1)S(1)}, s32[]{:S(2)}) async-start(s8[4423680]{0:T(1024)(128)(4,1)} %bitcast.205), calls=%async_computation | async-start | bytes 8388608
  165.2 2.3 copy-start.14
  165.2 6.3 %slice-start.1 = ((s8[4423680]{0:T(1024)(128)(4,1)}), s8[229376]{0:T(1024)(128)(4,1)S(1)}, s32[]{:S(2)}) async-start(s8[4423680]{0:T(1024)(128)(4,1)} %bitcast.205), calls=%async_computation.1 | async-start | bytes 458752
  167.5 4.1 %copy-start.5 = (f32[32,32,256]{2,1,0:T(8,128)S(1)}, f32[32,32,256]{2,1,0:T(8,128)}, u32[]{:S(2)}) copy-start(f32[32,32,256]{2,1,0:T(8,128)} %param.10) | copy-start | bytes 3145732
  167.5 4.1 %copy-start.8 = (pred[32,32,256]{2,1,0:T(8,128)(4,1)S(1)}, pred[32,32,256]{2,1,0:T(8,128)(4,1)}, u32[]{:S(2)}) copy-start(pred[32,32,256]{2,1,0:T(8,128)(4,1)} %copy-done.7) | copy-start | bytes 786436
  167.5 4.1 %copy-start.10 = (pred[32,32,256]{2,1,0:T(8,128)(4,1)S(1)}, pred[32,32,256]{2,1,0:T(8,128)(4,1)}, u32[]{:S(2)}) copy-start(pred[32,32,256]{2,1,0:T(8,128)(4,1)} %copy-done.9) | copy-start | bytes 786436
  167.5 4.1 %copy-start.12 = (pred[32,32,256]{2,1,0:T(8,128)(4,1)S(1)}, pred[32,32,256]{2,1,0:T(8,128)(4,1)}, u32[]{:S(2)}) copy-start(pred[32,32,256]{2,1,0:T(8,128)(4,1)} %copy-done.11) | copy-start | bytes 786436
  188.6 9.1 %copy-start.6 = (f32[3,32,32,256]{3,2,1,0:T(8,128)S(1)}, f32[3,32,32,256]{3,2,1,0:T(8,128)}, u32[]{:S(2)}) copy-start(f32[3,32,32,256]{3,2,1,0:T(8,128)} %param.9) | copy-start | bytes 9437188
where the time goes:
time: 292 us; the launch traced here: 291 us
  other arithmetic  142 us (49%)
  blocking collectives  75.3 us (26%)
  starting transfers between devices  25 us (9%)
  waiting for transfers between devices  19 us (7%)
  matrix products  15 us (5%)
  local copies, waits for them, and re-layouts  12.5 us (4%)
    unnamed x1, blocking collectives  75.3 us
    sub x2, other arithmetic, stencil(): SHIFT * center - rigidity_amount * laplace  71.8 us
    another operation x3, other arithmetic, stencil(): return jnp.stack(results)  26 us
    ppermute x4, starting transfers between devices, with_halo(): lax.ppermute(tail, axis, [(i, (i + 1) % count) for i in range(ends)])  19.7 us
    select_n x2, other arithmetic, solve_direct(): field = jnp.where(update, field + OMEGA * defect / scale, field)  15 us
    dot_general x1, matrix products, shards(): jnp.dot(vectors, residual_half.reshape(-1), preferred_element_type=jnp.fl...  14.3 us
    concatenate x4, other arithmetic, with_halo(): jnp.concatenate([lax.ppermute(tail, axis, [(i, (i + 1) % count) for i in...  12.4 us
    ppermute x4, waiting for transfers between devices, with_halo(): lax.ppermute(tail, axis, [(i, (i + 1) % count) for i in range(ends)])  11.4 us
  transfers between devices with their start and end apart: 8, of which 5 were waited for; matrix products, arithmetic and copies ran while one was open for 1% of the time, Pallas kernels for 0%

commit v1 on v0

v1 whole, which is shorter than its diff:
```python
import functools

import jax
import jax.numpy as jnp
from jax import lax
from jax.experimental import pallas as pl
from jax.experimental.pallas import tpu as pltpu
from jax.sharding import PartitionSpec as P

SHIFT = 1.0
ROBIN = 1.0
OMEGA = 0.6
MESH = pl.DeviceIdType.MESH

NX = 32
NY = 32
ROWS = 48
FIRST = 8
F32 = jnp.float32


def each(op, *pairs):
    return [op(*parts) for parts in zip(*pairs)]


def add(left, right):
    return each(lambda p, q: p + q, left, right)


def sub(left, right):
    return each(lambda p, q: p - q, left, right)


def mul(left, right):
    return each(lambda p, q: p * q, left, right)


def scaled(factor, pair):
    return [factor * part for part in pair]


def shifts(pair, lane):
    low, high = pair
    last = lane == 127
    first = lane == 0
    low_up = pltpu.roll(low, 127, 1)
    high_up = pltpu.roll(high, 127, 1)
    low_down = pltpu.roll(low, 1, 1)
    high_down = pltpu.roll(high, 1, 1)
    up = [jnp.where(last, high_up, low_up), jnp.where(last, 0.0, high_up)]
    down = [jnp.where(first, 0.0, low_down), jnp.where(first, low_down, high_down)]
    return up, down


def gap(pair, lane):
    up, down = shifts(pair, lane)
    return sub(up, down)


def block(field, forcing, mu, beta, x, yb, lane):
    row = FIRST + 8 * yb

    def at(component, dx, dy):
        return [field[component, x + 1 + dx, half, pl.ds(row + dy, 8), :] for half in (0, 1)]

    def own(ref):
        return [ref[x, pl.ds(8 * yb, 8), pl.ds(128 * half, 128)] for half in (0, 1)]

    shear, mixed = own(mu), own(beta)
    centre, ahead, behind, above, below = ([at(c, *o) for c in range(3)] for o in ((0, 0), (1, 0), (-1, 0), (0, 1), (0, -1)))
    turn = sub(ahead[0], behind[0])
    twist = sub(above[1], below[1])
    cross = [
        add(
            sub(sub(at(1, 1, 1), at(1, 1, -1)), sub(at(1, -1, 1), at(1, -1, -1))),
            gap(sub(ahead[2], behind[2]), lane),
        ),
        add(
            sub(sub(at(0, 1, 1), at(0, 1, -1)), sub(at(0, -1, 1), at(0, -1, -1))),
            gap(sub(above[2], below[2]), lane),
        ),
        gap(add(turn, twist), lane),
    ]
    defects = []
    for c in range(3):
        up, down = shifts(centre[c], lane)
        double = scaled(2.0, centre[c])
        seconds = [
            sub(add(ahead[c], behind[c]), double),
            sub(add(above[c], below[c]), double),
            sub(add(up, down), double),
        ]
        laplace = add(add(seconds[0], seconds[1]), seconds[2])
        graddiv = add(seconds[c], scaled(0.25, cross[c]))
        force = [forcing[c, x, pl.ds(8 * yb, 8), pl.ds(128 * half, 128)] for half in (0, 1)]
        defects.append(add(sub(force, centre[c]), add(mul(shear, laplace), mul(mixed, graddiv))))
    return centre, defects, shear, mixed


def kernel(
    deformation,
    traction,
    heat_level,
    label,
    table,
    span,
    basis,
    reciprocal,
    moved,
    residual,
    coarse,
    v0,
    v1,
    v2,
    force,
    heat,
    kind,
    mu,
    beta,
    kappa,
    vectors,
    rows_r,
    rimmed,
    side_send,
    side_recv,
    corner_send,
    corner_recv,
    total,
    line,
    near,
    far,
    load_sem,
    face_ss,
    face_rs,
    side_ss,
    side_rs,
    corner_ss,
    corner_rs,
    near_ss,
    near_rs,
    far_ss,
    far_rs,
):
    grp = lax.axis_index("grp")
    sub_at = lax.axis_index("sub")
    place = lax.rem(sub_at, 8)
    column = lax.div(sub_at, 8)
    cell = grp * 4 + column

    loads = [
        pltpu.make_async_copy(
            deformation.at[:, :, :, pl.ds(128 * half, 128)],
            v0.at[:, pl.ds(1, NX), half, pl.ds(FIRST, NY), :],
            load_sem.at[half],
        )
        for half in (0, 1)
    ]
    heat_load = pltpu.make_async_copy(heat_level, heat, load_sem.at[2])
    kind_load = pltpu.make_async_copy(label, kind, load_sem.at[3])
    force_load = pltpu.make_async_copy(traction, force, load_sem.at[4])
    rows_load = pltpu.make_async_copy(reciprocal, rows_r, load_sem.at[5])
    basis_load = pltpu.make_async_copy(basis, vectors, load_sem.at[6])
    for load in loads:
        load.start()
    heat_load.start()
    kind_load.start()
    force_load.start()

    def shifted(dx, dy):
        return (lax.rem(grp + 4 + dx, 4), lax.rem(sub_at + 32 + dy, 32))

    def near_peer(step):
        return (grp, column * 8 + lax.rem(place + step, 8))

    def far_peer(step):
        other = lax.rem(cell + step, 16)
        return (lax.div(other, 4), lax.rem(other, 4) * 8 + place)

    corners = ((-1, -1), (-1, 1), (1, -1), (1, 1))
    barrier = pltpu.get_barrier_semaphore()
    partners = [shifted(-1, 0), shifted(1, 0), shifted(0, -1), shifted(0, 1)]
    partners += [shifted(*corner) for corner in corners]
    partners += [near_peer(step) for step in range(1, 8)]
    partners += [far_peer(step) for step in range(1, 16)]
    for partner in partners:
        pl.semaphore_signal(barrier, inc=1, device_id=partner, device_id_type=MESH)

    lane = lax.broadcasted_iota(jnp.int32, (8, 128), 1)
    reach = span[0, 0]
    active = [lane < reach, lane + 128 < reach]

    def messages(round_at, field, low_face, high_face):
        found = []
        for side, dx in enumerate((-1, 1)):
            source = (low_face, high_face)[side]
            found.append(
                pltpu.make_async_remote_copy(
                    src_ref=source,
                    dst_ref=field.at[:, 33 if dx < 0 else 0, :, pl.ds(FIRST, NY), :],
                    send_sem=face_ss.at[round_at, side],
                    recv_sem=face_rs.at[round_at, side],
                    device_id=shifted(dx, 0),
                    device_id_type=MESH,
                )
            )
        for side, dy in enumerate((-1, 1)):
            found.append(
                pltpu.make_async_remote_copy(
                    src_ref=side_send.at[round_at, side],
                    dst_ref=side_recv.at[round_at, 1 - side],
                    send_sem=side_ss.at[round_at, side],
                    recv_sem=side_rs.at[round_at, side],
                    device_id=shifted(0, dy),
                    device_id_type=MESH,
                )
            )
        for number, corner in enumerate(corners):
            found.append(
                pltpu.make_async_remote_copy(
                    src_ref=corner_send.at[round_at, number],
                    dst_ref=corner_recv.at[round_at, 3 - number],
                    send_sem=corner_ss.at[round_at, number],
                    recv_sem=corner_rs.at[round_at, number],
                    device_id=shifted(*corner),
                    device_id_type=MESH,
                )
            )
        return found

    inside = [
        jnp.where(flag, 1.0, 0.0).astype(F32) for flag in (grp > 0, grp < 3, sub_at > 0, sub_at < 31)
    ]

    def pack_corners(round_at, take):
        for number, (dx, dy) in enumerate(corners):
            for c in range(3):
                for half in (0, 1):
                    corner_send[round_at, number, pl.ds(2 * c + half, 1), :] = take(dx, dy, c, half)

    def unpack(round_at, field):
        for c in range(3):
            for half in (0, 1):
                for number, (dx, dy) in enumerate(corners):
                    keep = inside[0 if dx < 0 else 1] * inside[2 if dy < 0 else 3]
                    field[c, 0 if dx < 0 else 33, half, pl.ds(7 if dy < 0 else 40, 1), :] = (
                        corner_recv[round_at, number, pl.ds(2 * c + half, 1), :] * keep
                    )

        @pl.loop(0, NX)
        def _(x):
            for side in (0, 1):
                for c in range(3):
                    for half in (0, 1):
                        field[c, x + 1, half, pl.ds(7 if side == 0 else 40, 1), :] = (
                            side_recv[round_at, side, c, half, pl.ds(x, 1), :] * inside[2 + side]
                        )

        for side in (0, 1):

            @pl.when(grp == (0 if side == 0 else 3))
            def _():
                field[:, 0 if side == 0 else 33, :, pl.ds(FIRST, NY), :] = jnp.zeros((3, 2, NY, 128), F32)

    def pack_side(round_at, field, x):
        for side in (0, 1):
            for c in range(3):
                for half in (0, 1):
                    side_send[round_at, side, c, half, pl.ds(x, 1), :] = field[
                        c, x + 1, half, pl.ds(FIRST if side == 0 else FIRST + NY - 1, 1), :
                    ]

    def field_corner(field):
        return lambda dx, dy, c, half: field[
            c, 1 if dx < 0 else NX, half, pl.ds(FIRST if dy < 0 else FIRST + NY - 1, 1), :
        ]

    def faces(field):
        return (
            field.at[:, 1, :, pl.ds(FIRST, NY), :],
            field.at[:, NX, :, pl.ds(FIRST, NY), :],
        )

    for load in loads:
        load.wait()
    basis_load.start()
    rows_load.start()

    @pl.loop(0, NX)
    def _(x):
        for c in range(3):
            for half in (0, 1):
                for yb in range(4):
                    rows = pl.ds(FIRST + 8 * yb, 8)
                    v0[c, x + 1, half, rows, :] = jnp.where(active[half], v0[c, x + 1, half, rows, :], 0.0)
        pack_side(0, v0, x)

    pack_corners(0, field_corner(v0))
    pl.semaphore_wait(barrier, len(partners))
    first = messages(0, v0, *faces(v0))
    for message in first:
        message.start()

    heat_load.wait()
    kind_load.wait()
    force_load.wait()

    @pl.loop(0, NX)
    def _(x):
        for yb in range(4):
            for half in (0, 1):
                at = (x, pl.ds(8 * yb, 8), pl.ds(128 * half, 128))
                material = kind[at]
                shear = jnp.full((8, 128), table[0, 0], F32)
                lame = jnp.full((8, 128), table[0, 1], F32)
                for number in range(1, 4):
                    chosen = material == number
                    shear = jnp.where(chosen, table[number, 0], shear)
                    lame = jnp.where(chosen, table[number, 1], lame)
                weakening = jnp.where(active[half], 2.0 - heat[at], 0.0)
                shear = shear * weakening
                mixed = lame * weakening + shear
                mu[at] = shear
                beta[at] = mixed
                kappa[at] = OMEGA / (SHIFT + 6.0 * shear + 2.0 * mixed)
                for c in range(3):
                    force[(c,) + at] = jnp.where(active[half], force[(c,) + at], 0.0)

    for message in first:
        message.wait_recv()
    unpack(0, v0)

    def sweep_block(source, target, x, yb, also_out):
        centre, defects, shear, mixed = block(source, force, mu, beta, x, yb, lane)
        step = [kappa[x, pl.ds(8 * yb, 8), pl.ds(128 * half, 128)] for half in (0, 1)]
        for c in range(3):
            new = add(centre[c], mul(step, defects[c]))
            for half in (0, 1):
                target[c, x + 1, half, pl.ds(FIRST + 8 * yb, 8), :] = new[half]
                if also_out:
                    moved[c, x, pl.ds(8 * yb, 8), pl.ds(128 * half, 128)] = new[half]
        return centre, defects, shear, mixed

    def first_edge(x, yb):
        slot = jnp.where(x == 0, 0, jnp.where(x == NX - 1, 1, 2))
        centre, defects, shear, mixed = sweep_block(v0, v1, x, yb, False)
        step = each(lambda p, q: OMEGA / (SHIFT + ROBIN + 6.0 * p + 2.0 * q), shear, mixed)
        for c in range(3):
            new = add(centre[c], mul(step, defects[c]))
            for half in (0, 1):
                rimmed[slot, c, half, pl.ds(8 * yb, 8), :] = new[half]

    @pl.loop(0, 2)
    def _(end):
        for yb in (1, 2):
            first_edge(end * (NX - 1), yb)

    @pl.loop(0, NX)
    def _(x):
        slot = jnp.where(x == 0, 0, jnp.where(x == NX - 1, 1, 2))
        for yb in (0, 3):
            first_edge(x, yb)
        for side in (0, 1):
            for c in range(3):
                for half in (0, 1):
                    side_send[1, side, c, half, pl.ds(x, 1), :] = rimmed[
                        slot, c, half, pl.ds(0 if side == 0 else NY - 1, 1), :
                    ]

    pack_corners(
        1,
        lambda dx, dy, c, half: rimmed[
            0 if dx < 0 else 1, c, half, pl.ds(0 if dy < 0 else NY - 1, 1), :
        ],
    )
    second = messages(1, v1, rimmed.at[0], rimmed.at[1])
    for message in second:
        message.start()

    @pl.loop(1, NX - 1)
    def _(x):
        for yb in (1, 2):
            sweep_block(v0, v1, x, yb, False)

    @pl.loop(1, NX - 1)
    def _(x):
        for yb in (1, 2):
            sweep_block(v1, v2, x, yb, True)

    for message in second:
        message.wait_recv()
    unpack(1, v1)

    @pl.loop(0, 2)
    def _(end):
        for yb in (1, 2):
            sweep_block(v1, v2, end * (NX - 1), yb, True)

    @pl.loop(0, NX)
    def _(x):
        for yb in (0, 3):
            sweep_block(v1, v2, x, yb, True)
        pack_side(2, v2, x)

    pack_corners(2, field_corner(v2))
    third = messages(2, v2, *faces(v2))
    for message in third:
        message.start()

    def residual_block(x, yb):
        _, defects, _, _ = block(v2, force, mu, beta, x, yb, lane)
        for c in range(3):
            for half in (0, 1):
                residual[c, x, pl.ds(8 * yb, 8), pl.ds(128 * half, 128)] = defects[c][half]

    @pl.loop(1, NX - 1)
    def _(x):
        for yb in (1, 2):
            residual_block(x, yb)

    for message in third:
        message.wait_recv()
    unpack(2, v2)
    basis_load.wait()
    total[...] = jnp.zeros_like(total)

    @pl.loop(0, 2)
    def _(end):
        for yb in (1, 2):
            residual_block(end * (NX - 1), yb)

    @pl.loop(0, NX)
    def _(x):
        for yb in (0, 3):
            residual_block(x, yb)
        part = total[...]
        for c in range(3):
            half_way = residual[c, x].astype(jnp.bfloat16)
            plane = vectors[:, c, x].reshape(8 * NY, 256)
            part += lax.dot_general(
                half_way, plane, (((1,), (1,)), ((), ())), preferred_element_type=F32
            )
        total[...] = part

    own_row = lax.broadcasted_iota(jnp.int32, (NY, 256), 0)
    of_lane = lax.broadcasted_iota(jnp.int32, (NY, 256), 1)
    kept = jnp.where(lax.rem(of_lane, NY) == own_row, total[...], 0.0)
    folded = kept[0:8] + kept[8:16] + kept[16:24] + kept[24:32]
    source_lane = lax.broadcasted_iota(jnp.int32, (256, 128), 0)
    target_lane = lax.broadcasted_iota(jnp.int32, (256, 128), 1)
    start_lane = 64 * lax.rem(cell, 2) + 8 * place
    pick = jnp.where(start_lane + lax.div(source_lane, NY) == target_lane, 1.0, 0.0).astype(F32)
    spread = jnp.dot(folded, pick, preferred_element_type=F32, precision=lax.Precision.HIGHEST)
    line[0] = jnp.sum(spread, axis=0, keepdims=True)

    hops = [
        pltpu.make_async_remote_copy(
            src_ref=line.at[0],
            dst_ref=near.at[step],
            send_sem=near_ss.at[step],
            recv_sem=near_rs.at[step],
            device_id=near_peer(step),
            device_id_type=MESH,
        )
        for step in range(1, 8)
    ]
    for hop in hops:
        hop.start()
    joined = line[0]
    rows_load.wait()
    for step, hop in enumerate(hops):
        hop.wait_recv()
        joined = joined + near[step + 1]
    line[1] = joined
    leaps = [
        pltpu.make_async_remote_copy(
            src_ref=line.at[1],
            dst_ref=far.at[step],
            send_sem=far_ss.at[step],
            recv_sem=far_rs.at[step],
            device_id=far_peer(step),
            device_id_type=MESH,
        )
        for step in range(1, 16)
    ]
    for leap in leaps:
        leap.start()

    def product(step, values):
        owner = lax.rem(cell + 16 - step, 16)
        columns = pl.ds(pl.multiple_of(lax.div(owner, 2) * 128, 128), 128)
        return rows_r[:, columns] * values

    answer = product(0, joined)
    for message in first + second + third:
        message.wait_send()
    for hop in hops:
        hop.wait_send()
    for step, leap in enumerate(leaps):
        leap.wait_recv()
        answer = answer + product(step + 1, far[step + 1])
    coarse[...] = jnp.broadcast_to(jnp.sum(answer, axis=1, keepdims=True), (8, 128))
    for leap in leaps:
        leap.wait_send()


def shards(
    deformation_vector,
    heating_traction,
    heat_level,
    substance_label,
    substance_stiffness_list,
    subregion_spans,
    projection_basis,
    reduced_system_reciprocal,
):
    hbm = pl.BlockSpec(memory_space=pltpu.HBM)
    vmem = pl.BlockSpec(memory_space=pltpu.VMEM)
    smem = pl.BlockSpec(memory_space=pltpu.SMEM)
    field = pltpu.VMEM((3, NX + 2, 2, ROWS, 128), F32)
    scalar = pltpu.VMEM((NX, NY, 256), F32)
    dma = pltpu.SemaphoreType.DMA
    moved, residual, coarse = pl.pallas_call(
        kernel,
        out_shape=(
            jax.ShapeDtypeStruct((3, NX, NY, 256), F32),
            jax.ShapeDtypeStruct((3, NX, NY, 256), F32),
            jax.ShapeDtypeStruct((8, 128), F32),
        ),
        in_specs=[hbm, hbm, hbm, hbm, smem, smem, hbm, hbm],
        out_specs=(vmem, vmem, vmem),
        scratch_shapes=[
            field,
            field,
            field,
            pltpu.VMEM((3, NX, NY, 256), F32),
            scalar,
            pltpu.VMEM((NX, NY, 256), jnp.int32),
            scalar,
            scalar,
            scalar,
            pltpu.VMEM((8, 3, NX, NY, 256), jnp.bfloat16),
            pltpu.VMEM((8, 1024), F32),
            pltpu.VMEM((3, 3, 2, NY, 128), F32),
            pltpu.VMEM((3, 2, 3, 2, NX, 128), F32),
            pltpu.VMEM((3, 2, 3, 2, NX, 128), F32),
            pltpu.VMEM((3, 4, 8, 128), F32),
            pltpu.VMEM((3, 4, 8, 128), F32),
            pltpu.VMEM((NY, 256), F32),
            pltpu.VMEM((2, 1, 128), F32),
            pltpu.VMEM((8, 1, 128), F32),
            pltpu.VMEM((16, 1, 128), F32),
            dma((7,)),
            dma((3, 2)),
            dma((3, 2)),
            dma((3, 2)),
            dma((3, 2)),
            dma((3, 4)),
            dma((3, 4)),
            dma((8,)),
            dma((8,)),
            dma((16,)),
            dma((16,)),
        ],
        compiler_params=pltpu.CompilerParams(
            collective_id=0, has_side_effects=True, vmem_limit_bytes=44 * 1024 * 1024
        ),
    )(
        deformation_vector,
        heating_traction,
        heat_level,
        substance_label,
        substance_stiffness_list,
        subregion_spans,
        projection_basis,
        reduced_system_reciprocal,
    )
    return moved, residual, coarse[:, 0]


def solution(mesh):
    placed = (
        P(None, "grp", "sub", None),
        P(None, "grp", "sub", None),
        P("grp", "sub", None),
        P("grp", "sub", None),
        P(),
        P("grp", "sub"),
        P(None, None, "grp", "sub", None),
        P(("grp", "sub"), None),
    )
    return jax.shard_map(
        shards,
        mesh=mesh,
        in_specs=placed,
        out_specs=(P(None, "grp", "sub", None), P(None, "grp", "sub", None), P(("grp", "sub"))),
        check_vma=False,
    )
```

time: 292 us -> 64.6 us (0.22)
  other arithmetic: 142 us -> 0 us
  blocking collectives: 75.3 us -> 0 us
  Pallas kernels: 0 us -> 55.1 us
  starting transfers between devices: 25 us -> 0 us
  waiting for transfers between devices: 19 us -> 0 us
  matrix products: 15 us -> 0 us
  local copies, waits for them, and re-layouts: 12.5 us -> 7.92 us
    unnamed x1 -> x0, blocking collectives: 75.3 us -> none
    sub x2 -> x0, other arithmetic: 71.8 us -> none  [stencil(): SHIFT * center - rigidity_amount * laplace]
    pallas_call x0 -> x1, Pallas kernels: none -> 55.1 us  [shards(): pl.pallas_call(kernel, out_shape=(jax.ShapeDtypeStruct((3, NX, NY, 256),...]
    another operation x3 -> x0, other arithmetic: 26 us -> none  [stencil(): return jnp.stack(results)]
    ppermute x8 -> x0, starting transfers between devices: 25 us -> none  [the longest x4 19.7 us: with_halo(): lax.ppermute(tail, axis, [(i, (i + 1) % count) for i in range(ends)])]
    select_n x4 -> x0, other arithmetic: 20 us -> none  [the longest x2 15 us: solve_direct(): field = jnp.where(update, field + OMEGA * defect / scale, field)]
    ppermute x8 -> x0, waiting for transfers between devices: 19 us -> none  [the longest x4 11.4 us: with_halo(): lax.ppermute(tail, axis, [(i, (i + 1) % count) for i in range(ends)])]
    dot_general x2 -> x0, matrix products: 15 us -> none  [the longest x1 14.3 us: shards(): jnp.dot(vectors, residual_half.reshape(-1), preferred_element_type=jnp.fl...]
  transfers between devices with their start and end apart: 8 -> 0, of which waited for: 5 -> 0; matrix products, arithmetic and copies ran while one was open for 1% -> 0% of each run, Pallas kernels for 0% -> 0%
where the time goes in v1:
time: 64.6 us; the launch traced here: 64.3 us
  Pallas kernels  55.1 us (85%)
  local copies, waits for them, and re-layouts  7.92 us (12%)
  between operations  1.29 us (2%)
    pallas_call x1, Pallas kernels, shards(): pl.pallas_call(kernel, out_shape=(jax.ShapeDtypeStruct((3, NX, NY, 256),...  55.1 us
    unnamed x9, local copies, waits for them, and re-layouts  7.3 us

profile of v1, /device:TPU:0, one launch (start us, length us, event | category | flops | bytes accessed | tf_op | source)
XLA Modules:
  0.0 64.3 jit_solution(3389528671631615590)
XLA Ops:
  1.3 0.8 %copy.12.table = f32[4,2]{1,0:T(4,128)S(1)} copy(f32[4,2]{0,1:T(2,128)} %param.12) | data formatting | bytes 64 | tf_op args[4]
  2.0 0.0 copy-start
  2.0 1.2 %copy-done = f32[32,32,256]{2,1,0:T(8,128)S(1)} copy-done((f32[32,32,256]{2,1,0:T(8,128)S(1)}, f32[32,32,256]{2,1,0:T(8,128)}, u32[]{:S(2)}) %copy-start) | copy-done | bytes 1048600
  3.3 0.0 copy-start.1
  3.3 1.2 %copy-done.1 = s32[32,32,256]{2,1,0:T(8,128)S(1)} copy-done((s32[32,32,256]{2,1,0:T(8,128)S(1)}, s32[32,32,256]{2,1,0:T(8,128)}, u32[]{:S(2)}) %copy-start.1) | copy-done | bytes 1048600
  4.5 0.0 copy-start.2
  4.5 0.8 %copy-done.2 = f32[8,1024]{1,0:T(8,128)S(1)} copy-done((f32[8,1024]{1,0:T(8,128)S(1)}, f32[8,1024]{1,0:T(8,128)}, u32[]{:S(2)}) %copy-start.2) | copy-done | bytes 32792
  5.3 55.1 %shard_map.103 = (f32[3,32,32,256]{3,2,1,0:T(8,128)S(1)}, f32[3,32,32,256]{3,2,1,0:T(8,128)S(1)}, f32[8,128]{1,0:T(8,128)S(1)}) custom-call(f32[3,32,32,256]{3,2,1,0:T(8,128)} %deformation.1, f32[3,32,32,256]{3,2,1,0:T(8,128)} %traction.1, f32[32,32,256]{2,1,0:T(8,128)S(1)} %copy-done, s32[32,32,256]{2,1,0:T(8,128)S(1)} %copy-done.1, ...), custom_call_target="tpu_custom_call" | custom-call | tf_op jit(solution)/shard_map/pallas_call | solution.py:522
  60.4 0.6 slice_reduce_fusion
  61.0 1.7 %copy.16 = f32[3,32,32,256]{3,2,1,0:T(8,128)} copy(f32[3,32,32,256]{3,2,1,0:T(8,128)S(1)} %get-tuple-element.12) | data formatting | bytes 6291456
  62.7 1.7 %copy.17 = f32[3,32,32,256]{3,2,1,0:T(8,128)} copy(f32[3,32,32,256]{3,2,1,0:T(8,128)S(1)} %get-tuple-element.13) | data formatting | bytes 6291456
Async XLA Ops:
  2.0 1.2 %copy-start = (f32[32,32,256]{2,1,0:T(8,128)S(1)}, f32[32,32,256]{2,1,0:T(8,128)}, u32[]{:S(2)}) copy-start(f32[32,32,256]{2,1,0:T(8,128)} %heat_level.1) | copy-start | bytes 3145732
  3.3 1.2 %copy-start.1 = (s32[32,32,256]{2,1,0:T(8,128)S(1)}, s32[32,32,256]{2,1,0:T(8,128)}, u32[]{:S(2)}) copy-start(s32[32,32,256]{2,1,0:T(8,128)} %label.1) | copy-start | bytes 3145732
  4.5 0.8 %copy-start.2 = (f32[8,1024]{1,0:T(8,128)S(1)}, f32[8,1024]{1,0:T(8,128)}, u32[]{:S(2)}) copy-start(f32[8,1024]{1,0:T(8,128)} %reciprocal.1) | copy-start | bytes 98308

commit v2 on v1

--- a/solution.py
+++ b/solution.py
@@ -16,6 +16,7 @@
 NY = 32
 ROWS = 48
 FIRST = 8
+BATCH = 8
 F32 = jnp.float32
 
 
@@ -39,62 +40,54 @@
     return [factor * part for part in pair]
 
 
-def shifts(pair, lane):
-    low, high = pair
-    last = lane == 127
-    first = lane == 0
-    low_up = pltpu.roll(low, 127, 1)
-    high_up = pltpu.roll(high, 127, 1)
-    low_down = pltpu.roll(low, 1, 1)
-    high_down = pltpu.roll(high, 1, 1)
-    up = [jnp.where(last, high_up, low_up), jnp.where(last, 0.0, high_up)]
-    down = [jnp.where(first, 0.0, low_down), jnp.where(first, low_down, high_down)]
-    return up, down
-
-
-def gap(pair, lane):
-    up, down = shifts(pair, lane)
-    return sub(up, down)
-
-
-def block(field, forcing, mu, beta, x, yb, lane):
+def block(field, slope, bend, forcing, mu, beta, x, yb):
     row = FIRST + 8 * yb
 
-    def at(component, dx, dy):
-        return [field[component, x + 1 + dx, half, pl.ds(row + dy, 8), :] for half in (0, 1)]
-
-    def own(ref):
-        return [ref[x, pl.ds(8 * yb, 8), pl.ds(128 * half, 128)] for half in (0, 1)]
+    def at(source, component, dx, dy):
+        return [source[component, x + 1 + dx, half, pl.ds(row + dy, 8), :] for half in (0, 1)]
+
+    def own(ref, *lead):
+        return [ref[(*lead, x, pl.ds(8 * yb, 8), pl.ds(128 * half, 128))] for half in (0, 1)]
 
     shear, mixed = own(mu), own(beta)
-    centre, ahead, behind, above, below = ([at(c, *o) for c in range(3)] for o in ((0, 0), (1, 0), (-1, 0), (0, 1), (0, -1)))
-    turn = sub(ahead[0], behind[0])
-    twist = sub(above[1], below[1])
-    cross = [
+    cross = []
+    for c, other in ((0, 1), (1, 0)):
+        turn = sub(
+            sub(at(field, other, 1, 1), at(field, other, 1, -1)),
+            sub(at(field, other, -1, 1), at(field, other, -1, -1)),
+        )
+        ends = ((1, 0), (-1, 0)) if c == 0 else ((0, 1), (0, -1))
+        lift = sub(at(slope, 2, *ends[0]), at(slope, 2, *ends[1]))
+        cross.append(add(scaled(0.25, turn), lift))
+    cross.append(
         add(
-            sub(sub(at(1, 1, 1), at(1, 1, -1)), sub(at(1, -1, 1), at(1, -1, -1))),
-            gap(sub(ahead[2], behind[2]), lane),
-        ),
-        add(
-            sub(sub(at(0, 1, 1), at(0, 1, -1)), sub(at(0, -1, 1), at(0, -1, -1))),
-            gap(sub(above[2], below[2]), lane),
-        ),
-        gap(add(turn, twist), lane),
-    ]
-    defects = []
+            sub(at(slope, 0, 1, 0), at(slope, 0, -1, 0)),
+            sub(at(slope, 1, 0, 1), at(slope, 1, 0, -1)),
+        )
+    )
+    centres, defects = [], []
     for c in range(3):
-        up, down = shifts(centre[c], lane)
-        double = scaled(2.0, centre[c])
-        seconds = [
-            sub(add(ahead[c], behind[c]), double),
-            sub(add(above[c], below[c]), double),
-            sub(add(up, down), double),
-        ]
-        laplace = add(add(seconds[0], seconds[1]), seconds[2])
-        graddiv = add(seconds[c], scaled(0.25, cross[c]))
-        force = [forcing[c, x, pl.ds(8 * yb, 8), pl.ds(128 * half, 128)] for half in (0, 1)]
-        defects.append(add(sub(force, centre[c]), add(mul(shear, laplace), mul(mixed, graddiv))))
-    return centre, defects, shear, mixed
+        centre = at(field, c, 0, 0)
+        across = add(at(field, c, 1, 0), at(field, c, -1, 0))
+        along = add(at(field, c, 0, 1), at(field, c, 0, -1))
+        rest = own(bend, c)
+        laplace = add(add(across, along), rest)
+        second = (
+            sub(across, scaled(2.0, centre)),
+            sub(along, scaled(2.0, centre)),
+            add(rest, scaled(4.0, centre)),
+        )[c]
+        graddiv = add(second, cross[c])
+        force = own(forcing, c)
+        defects.append(add(sub(force, centre), add(mul(shear, laplace), mul(mixed, graddiv))))
+        centres.append(centre)
+    return centres, defects, shear, mixed
+
+
+def along_z(values, matrix):
+    high = values.astype(jnp.bfloat16)
+    low = (values - high.astype(F32)).astype(jnp.bfloat16)
+    return jnp.dot(jnp.concatenate([high, low], axis=1), matrix, preferred_element_type=F32)
 
 
 def kernel(
@@ -102,7 +95,7 @@
     traction,
     heat_level,
     label,
-    table,
+    stiffness,
     span,
     basis,
     reciprocal,
@@ -112,10 +105,14 @@
     v0,
     v1,
     v2,
+    slope,
+    bend,
+    bands,
+    fringe,
+    table,
     force,
     heat,
     kind,
-    mu,
     beta,
     kappa,
     vectors,
@@ -147,6 +144,8 @@
     column = lax.div(sub_at, 8)
     cell = grp * 4 + column
 
+    mu = heat
+
     loads = [
         pltpu.make_async_copy(
             deformation.at[:, :, :, pl.ds(128 * half, 128)],
@@ -162,6 +161,8 @@
     basis_load = pltpu.make_async_copy(basis, vectors, load_sem.at[6])
     for load in loads:
         load.start()
+    table_load = pltpu.make_async_copy(stiffness, table, load_sem.at[7])
+    table_load.start()
     heat_load.start()
     kind_load.start()
     force_load.start()
@@ -188,6 +189,28 @@
     lane = lax.broadcasted_iota(jnp.int32, (8, 128), 1)
     reach = span[0, 0]
     active = [lane < reach, lane + 128 < reach]
+
+    above_diagonal = lax.broadcasted_iota(jnp.int32, (256, 256), 0) - lax.broadcasted_iota(jnp.int32, (256, 256), 1)
+    beside = jnp.where(jnp.abs(above_diagonal) == 1, 1.0, 0.0)
+    for part in (pl.ds(0, 256), pl.ds(256, 256)):
+        bands[part, 0:256] = jnp.where(above_diagonal == 0, -6.0, beside).astype(jnp.bfloat16)
+        bands[part, 256:512] = (0.25 * beside * above_diagonal.astype(F32)).astype(jnp.bfloat16)
+
+    def derive(field):
+        rows = pl.ds(FIRST, NY)
+
+        @pl.loop(0, NX // BATCH)
+        def _(batch):
+            at = [(c, BATCH * batch + number) for number in range(BATCH) for c in range(3)]
+            values = [
+                jnp.concatenate([field[c, x + 1, half, rows, :] for half in (0, 1)], axis=1) for c, x in at
+            ]
+            found = along_z(jnp.concatenate(values, axis=0), bands[...])
+            for number, (c, x) in enumerate(at):
+                part = found[NY * number : NY * (number + 1)]
+                bend[c, x] = part[:, 0:256]
+                for half in (0, 1):
+                    slope[c, x + 1, half, rows, :] = part[:, 256 + 128 * half : 384 + 128 * half]
 
     def messages(round_at, field, low_face, high_face):
         found = []
@@ -246,20 +269,49 @@
                         corner_recv[round_at, number, pl.ds(2 * c + half, 1), :] * keep
                     )
 
+        for side in (0, 1):
+
+            @pl.when(grp == (0 if side == 0 else 3))
+            def _():
+                field[:, 0 if side == 0 else 33, :, pl.ds(FIRST, NY), :] = jnp.zeros((3, 2, NY, 128), F32)
+
+        rows = pl.ds(FIRST, NY)
+        values = [
+            jnp.concatenate([field[c, plane, half, rows, :] for half in (0, 1)], axis=1)
+            for plane in (0, 33)
+            for c in (0, 2)
+        ]
+        values += [
+            jnp.concatenate([side_recv[round_at, side, c, half] for half in (0, 1)], axis=1)
+            for side in (0, 1)
+            for c in (1, 2)
+        ]
+        found = along_z(jnp.concatenate(values, axis=0), bands[:, 256:512])
+        number = 0
+        for plane in (0, 33):
+            for c in (0, 2):
+                for half in (0, 1):
+                    slope[c, plane, half, rows, :] = found[NY * number : NY * (number + 1), 128 * half : 128 * half + 128]
+                number += 1
+        for side in (0, 1):
+            for c in (1, 2):
+                for half in (0, 1):
+                    fringe[side, c - 1, half] = found[NY * number : NY * (number + 1), 128 * half : 128 * half + 128]
+                number += 1
+
         @pl.loop(0, NX)
         def _(x):
             for side in (0, 1):
-                for c in range(3):
-                    for half in (0, 1):
-                        field[c, x + 1, half, pl.ds(7 if side == 0 else 40, 1), :] = (
+                row = pl.ds(7 if side == 0 else 40, 1)
+                for half in (0, 1):
+                    for c in range(3):
+                        field[c, x + 1, half, row, :] = (
                             side_recv[round_at, side, c, half, pl.ds(x, 1), :] * inside[2 + side]
                         )
-
-        for side in (0, 1):
-
-            @pl.when(grp == (0 if side == 0 else 3))
-            def _():
-                field[:, 0 if side == 0 else 33, :, pl.ds(FIRST, NY), :] = jnp.zeros((3, 2, NY, 128), F32)
+                    for c in (1, 2):
+                        slope[c, x + 1, half, row, :] = (
+                            fringe[side, c - 1, half, pl.ds(x, 1), :] * inside[2 + side]
+                        )
 
     def pack_side(round_at, field, x):
         for side in (0, 1):
@@ -300,6 +352,9 @@
     for message in first:
         message.start()
 
+    derive(v0)
+
+    table_load.wait()
     heat_load.wait()
     kind_load.wait()
     force_load.wait()
@@ -311,11 +366,11 @@
                 at = (x, pl.ds(8 * yb, 8), pl.ds(128 * half, 128))
                 material = kind[at]
                 shear = jnp.full((8, 128), table[0, 0], F32)
-                lame = jnp.full((8, 128), table[0, 1], F32)
+                lame = jnp.full((8, 128), table[1, 0], F32)
                 for number in range(1, 4):
                     chosen = material == number
-                    shear = jnp.where(chosen, table[number, 0], shear)
-                    lame = jnp.where(chosen, table[number, 1], lame)
+                    shear = jnp.where(chosen, table[0, number], shear)
+                    lame = jnp.where(chosen, table[1, number], lame)
                 weakening = jnp.where(active[half], 2.0 - heat[at], 0.0)
                 shear = shear * weakening
                 mixed = lame * weakening + shear
@@ -330,7 +385,7 @@
     unpack(0, v0)
 
     def sweep_block(source, target, x, yb, also_out):
-        centre, defects, shear, mixed = block(source, force, mu, beta, x, yb, lane)
+        centre, defects, shear, mixed = block(source, slope, bend, force, mu, beta, x, yb)
         step = [kappa[x, pl.ds(8 * yb, 8), pl.ds(128 * half, 128)] for half in (0, 1)]
         for c in range(3):
             new = add(centre[c], mul(step, defects[c]))
@@ -381,6 +436,8 @@
         for yb in (1, 2):
             sweep_block(v0, v1, x, yb, False)
 
+    derive(v1)
+
     @pl.loop(1, NX - 1)
     def _(x):
         for yb in (1, 2):
@@ -406,50 +463,55 @@
     for message in third:
         message.start()
 
+    derive(v2)
+
+    basis_load.wait()
+    total[...] = jnp.zeros_like(total)
+
     def residual_block(x, yb):
-        _, defects, _, _ = block(v2, force, mu, beta, x, yb, lane)
+        _, defects, _, _ = block(v2, slope, bend, force, mu, beta, x, yb)
+        sums = [None] * 8
+        pair = pl.ds(16 * (yb // 2), 16)
+        upper = 8 * (yb % 2)
         for c in range(3):
             for half in (0, 1):
-                residual[c, x, pl.ds(8 * yb, 8), pl.ds(128 * half, 128)] = defects[c][half]
+                columns = pl.ds(128 * half, 128)
+                value = defects[c][half]
+                residual[c, x, pl.ds(8 * yb, 8), columns] = value
+                value = value.astype(jnp.bfloat16).astype(F32)
+                for k in range(8):
+                    vector = vectors[k, c, x, pair, columns].astype(F32)[upper : upper + 8]
+                    term = vector * value
+                    sums[k] = term if sums[k] is None else sums[k] + term
+        return sums
+
+    def gather_sums(found):
+        for k in range(8):
+            part = found[0][k]
+            for other in found[1:]:
+                part = part + other[k]
+            total[k] += part
 
     @pl.loop(1, NX - 1)
     def _(x):
-        for yb in (1, 2):
-            residual_block(x, yb)
+        gather_sums([residual_block(x, yb) for yb in (1, 2)])
 
     for message in third:
         message.wait_recv()
     unpack(2, v2)
-    basis_load.wait()
-    total[...] = jnp.zeros_like(total)
 
     @pl.loop(0, 2)
     def _(end):
-        for yb in (1, 2):
-            residual_block(end * (NX - 1), yb)
+        gather_sums([residual_block(end * (NX - 1), yb) for yb in (1, 2)])
 
     @pl.loop(0, NX)
     def _(x):
-        for yb in (0, 3):
-            residual_block(x, yb)
-        part = total[...]
-        for c in range(3):
-            half_way = residual[c, x].astype(jnp.bfloat16)
-            plane = vectors[:, c, x].reshape(8 * NY, 256)
-            part += lax.dot_general(
-                half_way, plane, (((1,), (1,)), ((), ())), preferred_element_type=F32
-            )
-        total[...] = part
-
-    own_row = lax.broadcasted_iota(jnp.int32, (NY, 256), 0)
-    of_lane = lax.broadcasted_iota(jnp.int32, (NY, 256), 1)
-    kept = jnp.where(lax.rem(of_lane, NY) == own_row, total[...], 0.0)
-    folded = kept[0:8] + kept[8:16] + kept[16:24] + kept[24:32]
-    source_lane = lax.broadcasted_iota(jnp.int32, (256, 128), 0)
-    target_lane = lax.broadcasted_iota(jnp.int32, (256, 128), 1)
+        gather_sums([residual_block(x, yb) for yb in (0, 3)])
+
     start_lane = 64 * lax.rem(cell, 2) + 8 * place
-    pick = jnp.where(start_lane + lax.div(source_lane, NY) == target_lane, 1.0, 0.0).astype(F32)
-    spread = jnp.dot(folded, pick, preferred_element_type=F32, precision=lax.Precision.HIGHEST)
+    spread = jnp.zeros((8, 128), F32)
+    for k in range(8):
+        spread = jnp.where(lane == start_lane + k, jnp.sum(total[k], axis=1, keepdims=True), spread)
     line[0] = jnp.sum(spread, axis=0, keepdims=True)
 
     hops = [
@@ -519,6 +581,10 @@
     field = pltpu.VMEM((3, NX + 2, 2, ROWS, 128), F32)
     scalar = pltpu.VMEM((NX, NY, 256), F32)
     dma = pltpu.SemaphoreType.DMA
+
+    def far(array):
+        return pltpu.with_memory_space_constraint(array, pltpu.HBM)
+
     moved, residual, coarse = pl.pallas_call(
         kernel,
         out_shape=(
@@ -526,16 +592,20 @@
             jax.ShapeDtypeStruct((3, NX, NY, 256), F32),
             jax.ShapeDtypeStruct((8, 128), F32),
         ),
-        in_specs=[hbm, hbm, hbm, hbm, smem, smem, hbm, hbm],
+        in_specs=[hbm, hbm, hbm, hbm, hbm, smem, hbm, hbm],
         out_specs=(vmem, vmem, vmem),
         scratch_shapes=[
             field,
             field,
             field,
+            field,
+            pltpu.VMEM((3, NX, NY, 256), F32),
+            pltpu.VMEM((512, 512), jnp.bfloat16),
+            pltpu.VMEM((2, 2, 2, NX, 128), F32),
+            pltpu.SMEM((2, 4), F32),
             pltpu.VMEM((3, NX, NY, 256), F32),
             scalar,
             pltpu.VMEM((NX, NY, 256), jnp.int32),
-            scalar,
             scalar,
             scalar,
             pltpu.VMEM((8, 3, NX, NY, 256), jnp.bfloat16),
@@ -545,11 +615,11 @@
             pltpu.VMEM((3, 2, 3, 2, NX, 128), F32),
             pltpu.VMEM((3, 4, 8, 128), F32),
             pltpu.VMEM((3, 4, 8, 128), F32),
-            pltpu.VMEM((NY, 256), F32),
+            pltpu.VMEM((8, 8, 128), F32),
             pltpu.VMEM((2, 1, 128), F32),
             pltpu.VMEM((8, 1, 128), F32),
             pltpu.VMEM((16, 1, 128), F32),
-            dma((7,)),
+            dma((8,)),
             dma((3, 2)),
             dma((3, 2)),
             dma((3, 2)),
@@ -562,17 +632,17 @@
             dma((16,)),
         ],
         compiler_params=pltpu.CompilerParams(
-            collective_id=0, has_side_effects=True, vmem_limit_bytes=44 * 1024 * 1024
+            collective_id=0, has_side_effects=True, vmem_limit_bytes=46 * 1024 * 1024
         ),
     )(
-        deformation_vector,
-        heating_traction,
-        heat_level,
-        substance_label,
-        substance_stiffness_list,
+        far(deformation_vector),
+        far(heating_traction),
+        far(heat_level),
+        far(substance_label),
+        far(substance_stiffness_list.T),
         subregion_spans,
-        projection_basis,
-        reduced_system_reciprocal,
+        far(projection_basis),
+        far(reduced_system_reciprocal),
     )
     return moved, residual, coarse[:, 0]
 

time: 64.6 us -> 48.6 us (0.75)
  Pallas kernels: 55.1 us -> 43.3 us
  local copies, waits for them, and re-layouts: 7.92 us -> 3.95 us
    pallas_call x1, Pallas kernels: 55.1 us -> 43.3 us  [shards(): pl.pallas_call(kernel, out_shape=(jax.ShapeDtypeStruct((3, NX, NY, 256),...]
    unnamed x9 -> x2, local copies, waits for them, and re-layouts: 7.3 us -> 3.33 us
where the time goes in v2:
time: 48.6 us; the launch traced here: 48.5 us
  Pallas kernels  43.3 us (89%)
  local copies, waits for them, and re-layouts  3.95 us (8%)
  between operations  1.29 us (3%)
    pallas_call x1, Pallas kernels, shards(): pl.pallas_call(kernel, out_shape=(jax.ShapeDtypeStruct((3, NX, NY, 256),...  43.3 us
    unnamed x2, local copies, waits for them, and re-layouts  3.33 us

profile of v2, /device:TPU:0, one launch (start us, length us, event | category | flops | bytes accessed | tf_op | source)
XLA Modules:
  0.0 48.5 jit_solution(3927076963106886028)
XLA Ops:
  1.3 43.3 %shard_map.103 = (f32[3,32,32,256]{3,2,1,0:T(8,128)S(1)}, f32[3,32,32,256]{3,2,1,0:T(8,128)S(1)}, f32[8,128]{1,0:T(8,128)S(1)}) custom-call(f32[3,32,32,256]{3,2,1,0:T(8,128)} %deformation.1, f32[3,32,32,256]{3,2,1,0:T(8,128)} %traction.1, f32[32,32,256]{2,1,0:T(8,128)} %heat_level.1, s32[32,32,256]{2,1,0:T(8,128)} %label.1, f32[2,4]{1,0:T(2,128)} %bitcast.1, ...), custom_call_target="tpu_custom_call" | custom-call | tf_op jit(solution)/shard_map/pallas_call | solution.py:588
  44.6 0.6 %slice_reduce_fusion = f32[8]{0:T(128)} fusion(f32[8,128]{1,0:T(8,128)S(1)} %get-tuple-element.8), kind=kLoop, calls=%fused_computation | loop fusion | bytes 64 | tf_op jit(solution)/shard_map/slice | solution.py:647
  45.2 1.7 %copy.14 = f32[3,32,32,256]{3,2,1,0:T(8,128)} copy(f32[3,32,32,256]{3,2,1,0:T(8,128)S(1)} %get-tuple-element.12) | data formatting | bytes 6291456
  46.9 1.7 %copy.15 = f32[3,32,32,256]{3,2,1,0:T(8,128)} copy(f32[3,32,32,256]{3,2,1,0:T(8,128)S(1)} %get-tuple-element.13) | data formatting | bytes 6291456

commit v3 on v2

--- a/solution.py
+++ b/solution.py
@@ -260,7 +260,36 @@
                 for half in (0, 1):
                     corner_send[round_at, number, pl.ds(2 * c + half, 1), :] = take(dx, dy, c, half)
 
-    def unpack(round_at, field):
+    def unpack_sides(round_at, field):
+        values = [
+            jnp.concatenate([side_recv[round_at, side, c, half] for half in (0, 1)], axis=1)
+            for side in (0, 1)
+            for c in (1, 2)
+        ]
+        found = along_z(jnp.concatenate(values, axis=0), bands[:, 256:512])
+        number = 0
+        for side in (0, 1):
+            for c in (1, 2):
+                for half in (0, 1):
+                    fringe[side, c - 1, half] = found[NY * number : NY * (number + 1), 128 * half : 128 * half + 128]
+                number += 1
+
+        @pl.loop(0, NX // 2)
+        def _(pair):
+            for x in (2 * pair, 2 * pair + 1):
+                for side in (0, 1):
+                    row = pl.ds(7 if side == 0 else 40, 1)
+                    for half in (0, 1):
+                        for c in range(3):
+                            field[c, x + 1, half, row, :] = (
+                                side_recv[round_at, side, c, half, pl.ds(x, 1), :] * inside[2 + side]
+                            )
+                        for c in (1, 2):
+                            slope[c, x + 1, half, row, :] = (
+                                fringe[side, c - 1, half, pl.ds(x, 1), :] * inside[2 + side]
+                            )
+
+    def unpack_faces(round_at, field):
         for c in range(3):
             for half in (0, 1):
                 for number, (dx, dy) in enumerate(corners):
@@ -268,7 +297,6 @@
                     field[c, 0 if dx < 0 else 33, half, pl.ds(7 if dy < 0 else 40, 1), :] = (
                         corner_recv[round_at, number, pl.ds(2 * c + half, 1), :] * keep
                     )
-
         for side in (0, 1):
 
             @pl.when(grp == (0 if side == 0 else 3))
@@ -280,11 +308,6 @@
             jnp.concatenate([field[c, plane, half, rows, :] for half in (0, 1)], axis=1)
             for plane in (0, 33)
             for c in (0, 2)
-        ]
-        values += [
-            jnp.concatenate([side_recv[round_at, side, c, half] for half in (0, 1)], axis=1)
-            for side in (0, 1)
-            for c in (1, 2)
         ]
         found = along_z(jnp.concatenate(values, axis=0), bands[:, 256:512])
         number = 0
@@ -293,25 +316,30 @@
                 for half in (0, 1):
                     slope[c, plane, half, rows, :] = found[NY * number : NY * (number + 1), 128 * half : 128 * half + 128]
                 number += 1
-        for side in (0, 1):
-            for c in (1, 2):
-                for half in (0, 1):
-                    fringe[side, c - 1, half] = found[NY * number : NY * (number + 1), 128 * half : 128 * half + 128]
-                number += 1
-
-        @pl.loop(0, NX)
-        def _(x):
-            for side in (0, 1):
-                row = pl.ds(7 if side == 0 else 40, 1)
-                for half in (0, 1):
-                    for c in range(3):
-                        field[c, x + 1, half, row, :] = (
-                            side_recv[round_at, side, c, half, pl.ds(x, 1), :] * inside[2 + side]
-                        )
-                    for c in (1, 2):
-                        slope[c, x + 1, half, row, :] = (
-                            fringe[side, c - 1, half, pl.ds(x, 1), :] * inside[2 + side]
-                        )
+
+    def edges(round_at, found, field, work):
+        for message in found[2:4]:
+            message.wait_recv()
+        unpack_sides(round_at, field)
+
+        @pl.loop(0, NX // 2 - 1)
+        def _(pair):
+            work(2 * pair + 1, (0, 3))
+            work(2 * pair + 2, (0, 3))
+
+        for message in found[0:2] + found[4:8]:
+            message.wait_recv()
+        unpack_faces(round_at, field)
+
+        @pl.loop(0, 2)
+        def _(end):
+            work(end * (NX - 1), (0, 1, 2, 3))
+
+    def interior(work):
+        @pl.loop(0, NX // 2 - 1)
+        def _(pair):
+            work(2 * pair + 1, (1, 2))
+            work(2 * pair + 2, (1, 2))
 
     def pack_side(round_at, field, x):
         for side in (0, 1):
@@ -346,10 +374,12 @@
                     v0[c, x + 1, half, rows, :] = jnp.where(active[half], v0[c, x + 1, half, rows, :], 0.0)
         pack_side(0, v0, x)
 
-    pack_corners(0, field_corner(v0))
     pl.semaphore_wait(barrier, len(partners))
     first = messages(0, v0, *faces(v0))
-    for message in first:
+    for message in first[:4]:
+        message.start()
+    pack_corners(0, field_corner(v0))
+    for message in first[4:]:
         message.start()
 
     derive(v0)
@@ -380,10 +410,6 @@
                 for c in range(3):
                     force[(c,) + at] = jnp.where(active[half], force[(c,) + at], 0.0)
 
-    for message in first:
-        message.wait_recv()
-    unpack(0, v0)
-
     def sweep_block(source, target, x, yb, also_out):
         centre, defects, shear, mixed = block(source, slope, bend, force, mu, beta, x, yb)
         step = [kappa[x, pl.ds(8 * yb, 8), pl.ds(128 * half, 128)] for half in (0, 1)]
@@ -395,25 +421,15 @@
                     moved[c, x, pl.ds(8 * yb, 8), pl.ds(128 * half, 128)] = new[half]
         return centre, defects, shear, mixed
 
-    def first_edge(x, yb):
+    def first_edge(x, blocks):
         slot = jnp.where(x == 0, 0, jnp.where(x == NX - 1, 1, 2))
-        centre, defects, shear, mixed = sweep_block(v0, v1, x, yb, False)
-        step = each(lambda p, q: OMEGA / (SHIFT + ROBIN + 6.0 * p + 2.0 * q), shear, mixed)
-        for c in range(3):
-            new = add(centre[c], mul(step, defects[c]))
-            for half in (0, 1):
-                rimmed[slot, c, half, pl.ds(8 * yb, 8), :] = new[half]
-
-    @pl.loop(0, 2)
-    def _(end):
-        for yb in (1, 2):
-            first_edge(end * (NX - 1), yb)
-
-    @pl.loop(0, NX)
-    def _(x):
-        slot = jnp.where(x == 0, 0, jnp.where(x == NX - 1, 1, 2))
-        for yb in (0, 3):
-            first_edge(x, yb)
+        for yb in blocks:
+            centre, defects, shear, mixed = sweep_block(v0, v1, x, yb, False)
+            step = each(lambda p, q: OMEGA / (SHIFT + ROBIN + 6.0 * p + 2.0 * q), shear, mixed)
+            for c in range(3):
+                new = add(centre[c], mul(step, defects[c]))
+                for half in (0, 1):
+                    rimmed[slot, c, half, pl.ds(8 * yb, 8), :] = new[half]
         for side in (0, 1):
             for c in range(3):
                 for half in (0, 1):
@@ -421,48 +437,41 @@
                         slot, c, half, pl.ds(0 if side == 0 else NY - 1, 1), :
                     ]
 
+    def first_rest(x, blocks):
+        for yb in blocks:
+            sweep_block(v0, v1, x, yb, False)
+
+    def second_rest(x, blocks):
+        for yb in blocks:
+            sweep_block(v1, v2, x, yb, True)
+
+    def second_edge(x, blocks):
+        second_rest(x, blocks)
+        pack_side(2, v2, x)
+
+    edges(0, first, v0, first_edge)
+    second = messages(1, v1, rimmed.at[0], rimmed.at[1])
+    for message in second[:4]:
+        message.start()
     pack_corners(
         1,
         lambda dx, dy, c, half: rimmed[
             0 if dx < 0 else 1, c, half, pl.ds(0 if dy < 0 else NY - 1, 1), :
         ],
     )
-    second = messages(1, v1, rimmed.at[0], rimmed.at[1])
-    for message in second:
+    for message in second[4:]:
         message.start()
 
-    @pl.loop(1, NX - 1)
-    def _(x):
-        for yb in (1, 2):
-            sweep_block(v0, v1, x, yb, False)
-
+    interior(first_rest)
     derive(v1)
-
-    @pl.loop(1, NX - 1)
-    def _(x):
-        for yb in (1, 2):
-            sweep_block(v1, v2, x, yb, True)
-
-    for message in second:
-        message.wait_recv()
-    unpack(1, v1)
-
-    @pl.loop(0, 2)
-    def _(end):
-        for yb in (1, 2):
-            sweep_block(v1, v2, end * (NX - 1), yb, True)
-
-    @pl.loop(0, NX)
-    def _(x):
-        for yb in (0, 3):
-            sweep_block(v1, v2, x, yb, True)
-        pack_side(2, v2, x)
-
+    interior(second_rest)
+    edges(1, second, v1, second_edge)
+    third = messages(2, v2, *faces(v2))
+    for message in third[:4]:
+        message.start()
     pack_corners(2, field_corner(v2))
-    third = messages(2, v2, *faces(v2))
-    for message in third:
+    for message in third[4:]:
         message.start()
-
     derive(v2)
 
     basis_load.wait()
@@ -492,21 +501,11 @@
                 part = part + other[k]
             total[k] += part
 
-    @pl.loop(1, NX - 1)
-    def _(x):
-        gather_sums([residual_block(x, yb) for yb in (1, 2)])
-
-    for message in third:
-        message.wait_recv()
-    unpack(2, v2)
-
-    @pl.loop(0, 2)
-    def _(end):
-        gather_sums([residual_block(end * (NX - 1), yb) for yb in (1, 2)])
-
-    @pl.loop(0, NX)
-    def _(x):
-        gather_sums([residual_block(x, yb) for yb in (0, 3)])
+    def residual_work(x, blocks):
+        gather_sums([residual_block(x, yb) for yb in blocks])
+
+    interior(residual_work)
+    edges(2, third, v2, residual_work)
 
     start_lane = 64 * lax.rem(cell, 2) + 8 * place
     spread = jnp.zeros((8, 128), F32)
@@ -560,9 +559,25 @@
     for step, leap in enumerate(leaps):
         leap.wait_recv()
         answer = answer + product(step + 1, far[step + 1])
-    coarse[...] = jnp.broadcast_to(jnp.sum(answer, axis=1, keepdims=True), (8, 128))
+    own_lane = lane == lax.broadcasted_iota(jnp.int32, (8, 128), 0)
+    coarse[...] = jnp.sum(
+        jnp.where(own_lane, jnp.sum(answer, axis=1, keepdims=True), 0.0), axis=0, keepdims=True
+    )
     for leap in leaps:
         leap.wait_send()
+
+
+def finish(moved, residual, coarse, moved_out, residual_out, coarse_out, store_sem):
+    stores = [
+        pltpu.make_async_copy(source.at[c], target.at[c], store_sem.at[number, c])
+        for number, (source, target) in enumerate(((moved, moved_out), (residual, residual_out)))
+        for c in range(3)
+    ]
+    for store in stores:
+        store.start()
+    coarse_out[...] = coarse[0, 0:8]
+    for store in stores:
+        store.wait()
 
 
 def shards(
@@ -590,7 +605,7 @@
         out_shape=(
             jax.ShapeDtypeStruct((3, NX, NY, 256), F32),
             jax.ShapeDtypeStruct((3, NX, NY, 256), F32),
-            jax.ShapeDtypeStruct((8, 128), F32),
+            jax.ShapeDtypeStruct((1, 128), F32),
         ),
         in_specs=[hbm, hbm, hbm, hbm, hbm, smem, hbm, hbm],
         out_specs=(vmem, vmem, vmem),
@@ -644,7 +659,18 @@
         far(projection_basis),
         far(reduced_system_reciprocal),
     )
-    return moved, residual, coarse[:, 0]
+    return pl.pallas_call(
+        finish,
+        out_shape=(
+            jax.ShapeDtypeStruct((3, NX, NY, 256), F32),
+            jax.ShapeDtypeStruct((3, NX, NY, 256), F32),
+            jax.ShapeDtypeStruct((8,), F32),
+        ),
+        in_specs=[vmem, vmem, vmem],
+        out_specs=(hbm, hbm, vmem),
+        scratch_shapes=[dma((2, 3))],
+        compiler_params=pltpu.CompilerParams(vmem_limit_bytes=1024 * 1024),
+    )(moved, residual, coarse)
 
 
 def solution(mesh):

time: 48.6 us -> 43.7 us (0.90)
  local copies, waits for them, and re-layouts: 3.95 us -> 0 us
  Pallas kernels: 43.3 us -> 42.3 us
    pallas_call x1, Pallas kernels: 43.3 us -> 39.1 us  [shards(): pl.pallas_call(kernel, out_shape=(jax.ShapeDtypeStruct((3, NX, NY, 256),...]
    unnamed x2 -> x0, local copies, waits for them, and re-layouts: 3.33 us -> none
    pallas_call x0 -> x1, Pallas kernels: none -> 3.23 us  [shards(): pl.pallas_call(finish, out_shape=(jax.ShapeDtypeStruct((3, NX, NY, 256),...]
    slice x1 -> x0, local copies, waits for them, and re-layouts: 0.63 us -> none  [shards(): return (moved, residual, coarse[:, 0])]
where the time goes in v3:
time: 43.7 us; the launch traced here: 43.6 us
  Pallas kernels  42.3 us (97%)
  between operations  1.29 us (3%)
    pallas_call x1, Pallas kernels, shards(): pl.pallas_call(kernel, out_shape=(jax.ShapeDtypeStruct((3, NX, NY, 256),...  39.1 us
    pallas_call x1, Pallas kernels, shards(): pl.pallas_call(finish, out_shape=(jax.ShapeDtypeStruct((3, NX, NY, 256),...  3.23 us

profile of v3, /device:TPU:0, one launch (start us, length us, event | category | flops | bytes accessed | tf_op | source)
XLA Modules:
  0.0 43.6 jit_solution(13316888884025489372)
XLA Ops:
  1.3 39.1 %shard_map.103 = (f32[3,32,32,256]{3,2,1,0:T(8,128)S(1)}, f32[3,32,32,256]{3,2,1,0:T(8,128)S(1)}, f32[1,128]{1,0:T(1,128)S(1)}) custom-call(f32[3,32,32,256]{3,2,1,0:T(8,128)} %deformation.1, f32[3,32,32,256]{3,2,1,0:T(8,128)} %traction.1, f32[32,32,256]{2,1,0:T(8,128)} %heat_level.1, s32[32,32,256]{2,1,0:T(8,128)} %label.1, f32[2,4]{1,0:T(2,128)} %bitcast.1, ...), custom_call_target="tpu_custom_call" | custom-call | tf_op jit(solution)/shard_map/pallas_call | solution.py:603
  40.4 3.2 %shard_map.104 = (f32[3,32,32,256]{3,2,1,0:T(8,128)}, f32[3,32,32,256]{3,2,1,0:T(8,128)}, f32[8]{0:T(128)}) custom-call(f32[3,32,32,256]{3,2,1,0:T(8,128)S(1)} %get-tuple-element.6.moved, f32[3,32,32,256]{3,2,1,0:T(8,128)S(1)} %get-tuple-element.7.residual, f32[1,128]{1,0:T(1,128)S(1)} %get-tuple-element.8.coarse), custom_call_target="tpu_custom_call" | custom-call | tf_op jit(solution)/shard_map/pallas_call | solution.py:662

commit v4 on v3

--- a/solution.py
+++ b/solution.py
@@ -11,6 +11,15 @@
 ROBIN = 1.0
 OMEGA = 0.6
 MESH = pl.DeviceIdType.MESH
+
+
+def far_first(sizes):
+    found = [(p, q) for p in range(sizes[0]) for q in range(sizes[1]) if p or q]
+    return sorted(found, key=lambda at: (-sum(min(d, size - d) for d, size in zip(at, sizes)), at))
+
+
+NEAR = far_first((4, 2))
+FAR = far_first((4, 4))
 
 NX = 32
 NY = 32
@@ -171,18 +180,20 @@
         return (lax.rem(grp + 4 + dx, 4), lax.rem(sub_at + 32 + dy, 32))
 
     def near_peer(step):
-        return (grp, column * 8 + lax.rem(place + step, 8))
+        dy, dc = NEAR[step]
+        other = lax.rem(lax.div(place, 2) + dy, 4) * 2 + lax.rem(place + dc, 2)
+        return (grp, column * 8 + other)
 
     def far_peer(step):
-        other = lax.rem(cell + step, 16)
-        return (lax.div(other, 4), lax.rem(other, 4) * 8 + place)
+        dz, dx = FAR[step]
+        return (lax.rem(grp + dz, 4), lax.rem(column + dx, 4) * 8 + place)
 
     corners = ((-1, -1), (-1, 1), (1, -1), (1, 1))
     barrier = pltpu.get_barrier_semaphore()
     partners = [shifted(-1, 0), shifted(1, 0), shifted(0, -1), shifted(0, 1)]
     partners += [shifted(*corner) for corner in corners]
-    partners += [near_peer(step) for step in range(1, 8)]
-    partners += [far_peer(step) for step in range(1, 16)]
+    partners += [near_peer(step) for step in range(7)]
+    partners += [far_peer(step) for step in range(15)]
     for partner in partners:
         pl.semaphore_signal(barrier, inc=1, device_id=partner, device_id_type=MESH)
 
@@ -274,20 +285,18 @@
                     fringe[side, c - 1, half] = found[NY * number : NY * (number + 1), 128 * half : 128 * half + 128]
                 number += 1
 
-        @pl.loop(0, NX // 2)
-        def _(pair):
-            for x in (2 * pair, 2 * pair + 1):
-                for side in (0, 1):
-                    row = pl.ds(7 if side == 0 else 40, 1)
-                    for half in (0, 1):
-                        for c in range(3):
-                            field[c, x + 1, half, row, :] = (
-                                side_recv[round_at, side, c, half, pl.ds(x, 1), :] * inside[2 + side]
-                            )
-                        for c in (1, 2):
-                            slope[c, x + 1, half, row, :] = (
-                                fringe[side, c - 1, half, pl.ds(x, 1), :] * inside[2 + side]
-                            )
+    def unpack_rows(round_at, field, x):
+        for side in (0, 1):
+            row = pl.ds(7 if side == 0 else 40, 1)
+            for half in (0, 1):
+                for c in range(3):
+                    field[c, x + 1, half, row, :] = (
+                        side_recv[round_at, side, c, half, pl.ds(x, 1), :] * inside[2 + side]
+                    )
+                for c in (1, 2):
+                    slope[c, x + 1, half, row, :] = (
+                        fringe[side, c - 1, half, pl.ds(x, 1), :] * inside[2 + side]
+                    )
 
     def unpack_faces(round_at, field):
         for c in range(3):
@@ -321,9 +330,13 @@
         for message in found[2:4]:
             message.wait_recv()
         unpack_sides(round_at, field)
+        unpack_rows(round_at, field, 0)
+        unpack_rows(round_at, field, 1)
 
         @pl.loop(0, NX // 2 - 1)
         def _(pair):
+            unpack_rows(round_at, field, 2 * pair + 2)
+            unpack_rows(round_at, field, 2 * pair + 3)
             work(2 * pair + 1, (0, 3))
             work(2 * pair + 2, (0, 3))
 
@@ -449,6 +462,7 @@
         second_rest(x, blocks)
         pack_side(2, v2, x)
 
+    interior(first_rest)
     edges(0, first, v0, first_edge)
     second = messages(1, v1, rimmed.at[0], rimmed.at[1])
     for message in second[:4]:
@@ -462,7 +476,6 @@
     for message in second[4:]:
         message.start()
 
-    interior(first_rest)
     derive(v1)
     interior(second_rest)
     edges(1, second, v1, second_edge)
@@ -522,7 +535,7 @@
             device_id=near_peer(step),
             device_id_type=MESH,
         )
-        for step in range(1, 8)
+        for step in range(7)
     ]
     for hop in hops:
         hop.start()
@@ -530,7 +543,7 @@
     rows_load.wait()
     for step, hop in enumerate(hops):
         hop.wait_recv()
-        joined = joined + near[step + 1]
+        joined = joined + near[step]
     line[1] = joined
     leaps = [
         pltpu.make_async_remote_copy(
@@ -541,24 +554,25 @@
             device_id=far_peer(step),
             device_id_type=MESH,
         )
-        for step in range(1, 16)
+        for step in range(15)
     ]
     for leap in leaps:
         leap.start()
 
-    def product(step, values):
-        owner = lax.rem(cell + 16 - step, 16)
+    def product(offset, values):
+        dz, dx = offset
+        owner = lax.rem(grp + 4 - dz, 4) * 4 + lax.rem(column + 4 - dx, 4)
         columns = pl.ds(pl.multiple_of(lax.div(owner, 2) * 128, 128), 128)
         return rows_r[:, columns] * values
 
-    answer = product(0, joined)
+    answer = product((0, 0), joined)
     for message in first + second + third:
         message.wait_send()
     for hop in hops:
         hop.wait_send()
     for step, leap in enumerate(leaps):
         leap.wait_recv()
-        answer = answer + product(step + 1, far[step + 1])
+        answer = answer + product(FAR[step], far[step])
     own_lane = lane == lax.broadcasted_iota(jnp.int32, (8, 128), 0)
     coarse[...] = jnp.sum(
         jnp.where(own_lane, jnp.sum(answer, axis=1, keepdims=True), 0.0), axis=0, keepdims=True

time: 43.7 us -> 43.5 us (level)
  no operation moved by 1% of the time
where the time goes in v4:
time: 43.5 us; the launch traced here: 43.3 us
  Pallas kernels  42.1 us (97%)
  between operations  1.29 us (3%)
    pallas_call x1, Pallas kernels, shards(): pl.pallas_call(kernel, out_shape=(jax.ShapeDtypeStruct((3, NX, NY, 256),...  38.8 us
    pallas_call x1, Pallas kernels, shards(): pl.pallas_call(finish, out_shape=(jax.ShapeDtypeStruct((3, NX, NY, 256),...  3.23 us

profile of v4, /device:TPU:0, one launch (start us, length us, event | category | flops | bytes accessed | tf_op | source)
XLA Modules:
  0.0 43.3 jit_solution(3975673751702580055)
XLA Ops:
  1.3 38.8 %shard_map.103 = (f32[3,32,32,256]{3,2,1,0:T(8,128)S(1)}, f32[3,32,32,256]{3,2,1,0:T(8,128)S(1)}, f32[1,128]{1,0:T(1,128)S(1)}) custom-call(f32[3,32,32,256]{3,2,1,0:T(8,128)} %deformation.1, f32[3,32,32,256]{3,2,1,0:T(8,128)} %traction.1, f32[32,32,256]{2,1,0:T(8,128)} %heat_level.1, s32[32,32,256]{2,1,0:T(8,128)} %label.1, f32[2,4]{1,0:T(2,128)} %bitcast.1, ...), custom_call_target="tpu_custom_call" | custom-call | tf_op jit(solution)/shard_map/pallas_call | solution.py:617
  40.1 3.2 %shard_map.104 = (f32[3,32,32,256]{3,2,1,0:T(8,128)}, f32[3,32,32,256]{3,2,1,0:T(8,128)}, f32[8]{0:T(128)}) custom-call(f32[3,32,32,256]{3,2,1,0:T(8,128)S(1)} %get-tuple-element.6.moved, f32[3,32,32,256]{3,2,1,0:T(8,128)S(1)} %get-tuple-element.7.residual, f32[1,128]{1,0:T(1,128)S(1)} %get-tuple-element.8.coarse), custom_call_target="tpu_custom_call" | custom-call | tf_op jit(solution)/shard_map/pallas_call | solution.py:676
